TPU v7x, 128 devices: a whole 4x4x4 slice. The times are simulated.
128 devices in a mesh: tok: 8 (over y, z_lo), voc: 16 (over x, z_hi, core).
Axes of the slice: x: 4, y: 4, z: 4 (z_hi: 2, z_lo: 2; z = z_hi * 2 + z_lo), core: 2. Of those that a mesh axis runs over, the one named last changes fastest.
Arguments:
- hidden_states: bfloat16 [1024, 3584], P('tok'), may hold values from -18 to 18
- final_gain: float32 [3584], replicated, may hold values from 0.5 to 1.5
- student_head: bfloat16 [131072, 3584], P(('tok', 'voc')), may hold values from -2 to 2
- teacher_states: bfloat16 [1024, 4608], P('tok'), may hold values from -18 to 18
- teacher_head: bfloat16 [131072, 4608], P(('tok', 'voc')), may hold values from -2 to 2
- token_weight: float32 [1024], replicated, may hold values from 8 to 64
Outputs:
- states_grad: float32 [1024, 3584], P(('tok', 'voc'))
- gain_grad: float32 [3584], replicated
All inputs are finite; a program needn't handle non-finite values.
Results may differ from a plain program's by a relative error of at most 0.006.
Values may be sent and summed in bfloat16 or wider, within the bound.
No kernel may reach another device: no remote copies, remote signals or barrier semaphores. Data moves between devices by JAX's collectives and lax.ppermute only.
A program may use at most 128 MiB of HBM per device.

v0:
```python
import functools

import jax
import jax.numpy as jnp
from jax import lax
from jax.experimental import pallas as pl
from jax.experimental.pallas import tpu as pltpu
from jax.sharding import Mesh, PartitionSpec as P

EPSILON = 1e-06
AXES = ("y", "zl", "x", "zh", "c")
SIZES = (4, 2, 4, 2, 2)
F32 = jnp.float32
BF16 = jnp.bfloat16
STREAMED = 58 * 2**20
LARGE = 30 * 2**20
SMALL = 3 * 2**20


def place(y, z, x, c):
    y, z, x, c = y % 4, z % 4, x % 4, c % 2
    return (((y * 2 + z % 2) * 4 + x) * 2 + z // 2) * 2 + c


def permute(array, target):
    pairs = [
        (place(y, z, x, c), place(*target(y, z, x, c)))
        for y in range(4)
        for z in range(4)
        for x in range(4)
        for c in range(2)
    ]
    return lax.ppermute(array, AXES, pairs)


def moved(axis, steps):
    def target(y, z, x, c):
        by = steps if c == 0 else -steps
        name = axis[c]
        return (y + by * (name == "y"), z + by * (name == "z"), x + by * (name == "x"), c)

    return target


def pick(rows, columns):
    return rows[:, None] == lax.broadcasted_iota(jnp.int32, (rows.shape[0], columns), 1)


def row_parts(count, *sizes):
    index = lax.iota(jnp.int32, count)
    digits = []
    for size in reversed(sizes):
        digits.append(index % size)
        index = index // size
    return digits[::-1]


def columns_to_rows(columns):
    rows = columns[0].shape[0]
    wide = jnp.concatenate(
        columns + [jnp.zeros((rows, 128 - len(columns)), F32)], axis=1
    )
    return wide.T[:8]


def rows_to_columns(rows):
    count = rows.shape[1]
    return jnp.concatenate([rows, jnp.zeros((120, count), F32)], axis=0).T


def resident_kernel(*refs):
    count = (len(refs) - 1) // 2
    sem = refs[-1]
    copies = [
        pltpu.make_async_copy(refs[n], refs[count + n], sem.at[n]) for n in range(count)
    ]
    for copy in copies:
        copy.start()
    for copy in copies:
        copy.wait()


def resident(*arrays):
    return pl.pallas_call(
        resident_kernel,
        in_specs=[pl.BlockSpec(memory_space=pl.ANY)] * len(arrays),
        out_specs=[pl.BlockSpec(memory_space=pltpu.VMEM)] * len(arrays),
        out_shape=[pltpu.VMEM(array.shape, array.dtype) for array in arrays],
        scratch_shapes=[pltpu.SemaphoreType.DMA((len(arrays),))],
        compiler_params=pltpu.CompilerParams(vmem_limit_bytes=SMALL),
        cost_estimate=pl.CostEstimate(
            flops=0, bytes_accessed=4 * sum(a.size for a in arrays), transcendentals=0
        ),
    )(*[pltpu.with_memory_space_constraint(array, pltpu.HBM) for array in arrays])


def logits_kernel(tile, *refs):
    blocks, refs = refs[:-12], refs[-12:]
    gain, own_t, own_s, other_t, other_s, out_t, out_s, lse, normed, states_t, wait, sem = refs
    rows, vocab, dt = blocks[0].shape[0], own_t.shape[0], own_t.shape[1]
    slots = wait.shape[0]
    copies = [
        pltpu.make_async_copy(
            head.at[pl.ds(first, tile)], wait.at[n % slots], sem.at[n % slots]
        )
        for n, (head, first) in enumerate(
            (head, first) for head in (own_t, other_t) for first in range(0, vocab, tile)
        )
    ]
    for n in range(slots):
        copies[n].start()
    for k in range(4):
        span = pl.ds(k * rows, rows)
        block = blocks[k]
        states_t[span, :] = block[:, :dt]
        wide = (block[:, dt:] if block.shape[1] > dt else blocks[4][...]).astype(F32)
        inverse = lax.rsqrt(jnp.mean(wide * wide, axis=1, keepdims=True) + EPSILON)
        normed[span, :] = (wide * inverse * gain[...]).astype(BF16)
    count = states_t.shape[0]

    def statistics(out, n, top, total):
        part = out[:, pl.ds(n * tile, tile)]
        new = jnp.maximum(top, jnp.max(part, axis=1, keepdims=True))
        total = total * jnp.exp(top - new) + jnp.sum(
            jnp.exp(part - new), axis=1, keepdims=True
        )
        return new, total

    sums = []
    for states, out in ((normed, out_s), (states_t, out_t)):
        top = jnp.full((count, 1), -jnp.inf, F32)
        total = jnp.zeros((count, 1), F32)
        for n in range(2 * vocab // tile):
            if out is out_s:
                head = (own_s, other_s)[n * tile // vocab]
                head = head[pl.ds(n * tile % vocab, tile), :]
            else:
                copies[n].wait()
                head = wait[n % slots]
            out[:, pl.ds(n * tile, tile)] = lax.dot_general(
                states[...], head, (((1,), (1,)), ((), ())), preferred_element_type=F32
            )
            if out is out_t and n + slots < len(copies):
                copies[n + slots].start()
            if n:
                top, total = statistics(out, n - 1, top, total)
        top, total = statistics(out, 2 * vocab // tile - 1, top, total)
        sums.append(top + jnp.log(total))
    lse[...] = columns_to_rows(sums[::-1])


def streamed_kernel(tile, *refs):
    blocks, (gain, own_t, own_s, other_t, other_s) = refs[:4], refs[4:9]
    out_t, out_s, lse, normed, states_t, wait_t, wait_s, sem = refs[9:]
    rows, dt, vocab = blocks[0].shape[0], states_t.shape[1], own_t.shape[0]
    slots = wait_t.shape[0]
    work = []
    for pair, base in (((own_t, own_s), 0), ((other_t, other_s), vocab)):
        for kind in range(2):
            for first in range(0, vocab, tile):
                work.append((kind, pair[kind], first, base + first))
    copies, slot, used = [], [], [0, 0]
    for kind, head, first, _ in work:
        slot.append(used[kind] % slots)
        used[kind] += 1
        copies.append(
            pltpu.make_async_copy(
                head.at[pl.ds(first, tile)],
                (wait_t, wait_s)[kind].at[slot[-1]],
                sem.at[kind, slot[-1]],
            )
        )
    ahead = slots - 1
    for k in range(ahead):
        copies[k].start()
    for k, block in enumerate(blocks):
        span = pl.ds(k * rows, rows)
        states_t[span, :] = block[:, :dt]
        wide = block[:, dt:].astype(F32)
        inverse = lax.rsqrt(jnp.mean(wide * wide, axis=1, keepdims=True) + EPSILON)
        normed[span, :] = (wide * inverse * gain[...]).astype(BF16)
    count = states_t.shape[0]
    top = [jnp.full((count, 1), -jnp.inf, F32)] * 2
    total = [jnp.zeros((count, 1), F32)] * 2
    outs = (out_t, out_s)

    def statistics(k):
        kind, _, _, base = work[k]
        part = outs[kind][:, pl.ds(base, tile)]
        new = jnp.maximum(top[kind], jnp.max(part, axis=1, keepdims=True))
        total[kind] = total[kind] * jnp.exp(top[kind] - new) + jnp.sum(
            jnp.exp(part - new), axis=1, keepdims=True
        )
        top[kind] = new

    for k, (kind, _, _, base) in enumerate(work):
        copies[k].wait()
        if k + ahead < len(work):
            copies[k + ahead].start()
        outs[kind][:, pl.ds(base, tile)] = lax.dot_general(
            (states_t, normed)[kind][...],
            (wait_t, wait_s)[kind][slot[k]],
            (((1,), (1,)), ((), ())),
            preferred_element_type=F32,
        )
        if k:
            statistics(k - 1)
    statistics(len(work) - 1)
    lse[...] = columns_to_rows([t + jnp.log(z) for t, z in zip(top, total)])


def logits_streamed(blocks, gain, own_t, own_s, other_t, other_s):
    count = 4 * blocks[0].shape[0]
    vocab, dt = own_t.shape
    ds = own_s.shape[1]
    tile, slots = 512, 3
    vmem = pl.BlockSpec(memory_space=pltpu.VMEM)
    anywhere = pl.BlockSpec(memory_space=pl.ANY)
    return pl.pallas_call(
        functools.partial(streamed_kernel, tile),
        in_specs=[vmem] * 5 + [anywhere] * 4,
        out_specs=[vmem] * 4,
        out_shape=[
            jax.ShapeDtypeStruct((count, 2 * vocab), F32),
            jax.ShapeDtypeStruct((count, 2 * vocab), F32),
            jax.ShapeDtypeStruct((8, count), F32),
            jax.ShapeDtypeStruct((count, ds), BF16),
        ],
        scratch_shapes=[
            pltpu.VMEM((count, dt), BF16),
            pltpu.VMEM((slots, tile, dt), BF16),
            pltpu.VMEM((slots, tile, ds), BF16),
            pltpu.SemaphoreType.DMA((2, slots)),
        ],
        compiler_params=pltpu.CompilerParams(vmem_limit_bytes=STREAMED),
        cost_estimate=pl.CostEstimate(
            flops=4 * count * vocab * (dt + ds),
            bytes_accessed=4 * vocab * (dt + ds),
            transcendentals=4 * vocab * count,
        ),
    )(*blocks, gain, own_t, own_s, other_t, other_s)


def held(array):
    return pltpu.with_memory_space_constraint(array, pltpu.VMEM)


def logits(blocks, gain, own_t, own_s, other_t, other_s):
    count = 4 * blocks[0].shape[0]
    vocab, dt = own_t.shape
    ds = own_s.shape[1]
    tile, slots = 512, 2
    vmem = pl.BlockSpec(memory_space=pltpu.VMEM)
    anywhere = pl.BlockSpec(memory_space=pl.ANY)
    return pl.pallas_call(
        functools.partial(logits_kernel, tile),
        in_specs=[vmem] * (len(blocks) + 1) + [anywhere, vmem] * 2,
        out_specs=[vmem] * 4,
        out_shape=[
            jax.ShapeDtypeStruct((count, 2 * vocab), F32),
            jax.ShapeDtypeStruct((count, 2 * vocab), F32),
            jax.ShapeDtypeStruct((8, count), F32),
            jax.ShapeDtypeStruct((count, ds), BF16),
        ],
        scratch_shapes=[
            pltpu.VMEM((count, dt), BF16),
            pltpu.VMEM((slots, tile, dt), BF16),
            pltpu.SemaphoreType.DMA((slots,)),
        ],
        compiler_params=pltpu.CompilerParams(vmem_limit_bytes=LARGE),
        cost_estimate=pl.CostEstimate(
            flops=4 * count * vocab * (dt + ds),
            bytes_accessed=4 * vocab * (dt + ds),
            transcendentals=4 * vocab * count,
        ),
    )(*blocks, gain, own_t, held(own_s), other_t, held(other_s))


def backward_kernel(tile, later, *refs):
    teacher, student, normed, rows, gain, own, other = refs[:7]
    before = refs[7] if later else None
    refs = refs[7 + later :]
    sends_a, kept_a, refs = refs[:3], refs[3], refs[4:]
    outs_b, (gain_out, grad) = refs[:2], refs[2:]
    half, vocab = teacher.shape
    part, ds = own.shape
    steps = ds // tile
    columns = rows_to_columns(rows[...])
    lse_t, lse_s, weight = (columns[:, k : k + 1] for k in range(3))
    for first in range(0, vocab, 512):
        at = pl.ds(first, 512)
        gap = jnp.exp(student[:, at] - lse_s) - jnp.exp(teacher[:, at] - lse_t)
        grad[:, at] = (weight * gap).astype(BF16)
    for k in range(steps):
        at = pl.ds(k * tile, tile)
        out = jnp.dot(grad[:, :part], own[:, at], preferred_element_type=F32)
        out += jnp.dot(grad[:, part:], other[:, at], preferred_element_type=F32)
        share = jnp.sum(out * normed[:, at].astype(F32), axis=0, keepdims=True)
        share /= gain[:, at]
        gain_out[:, at] = share + before[:, at] if later else share
        second = k >= steps // 2
        at = pl.ds((k - second * (steps // 2)) * tile, tile)
        if second:
            for n in range(2):
                outs_b[n][:, at] = out[n * half // 2 : (n + 1) * half // 2].astype(
                    outs_b[n].dtype
                )
        else:
            for s in range(4):
                groups = [
                    out[64 * j + 16 * s : 64 * j + 16 * s + 16] for j in range(half // 64)
                ]
                piece = jnp.concatenate(groups, axis=0)
                if s == 0:
                    kept_a[:, at] = piece
                else:
                    sends_a[s - 1][pl.ds(0, half // 4), at] = piece.astype(BF16)
    if later:
        share = gain_out[...]
        high = share.astype(BF16).astype(F32)
        low = share - high
        tail = [p[:, n * ds // 2 : (n + 1) * ds // 2] for n in range(2) for p in (high, low)]
        tail = jnp.concatenate(tail + [jnp.zeros((12, ds // 2), F32)], axis=0).astype(BF16)
        for send in sends_a:
            send[pl.ds(half // 4, 16), :] = tail


def backward(part_of, rows, gain, own, other, before=None):
    teacher, student, _, normed = part_of
    later = before is not None
    half, vocab = teacher.shape
    part, ds = own.shape
    tile = ds // 4
    count = half // 4
    vmem = pl.BlockSpec(memory_space=pltpu.VMEM)
    wide = ds // 2
    out = pl.pallas_call(
        functools.partial(backward_kernel, tile, later),
        in_specs=[vmem] * (7 + later),
        out_specs=[vmem] * 7,
        out_shape=[jax.ShapeDtypeStruct((count + 16 * later, wide), BF16)] * 3
        + [jax.ShapeDtypeStruct((count, wide), F32)]
        + [jax.ShapeDtypeStruct((2 * count, wide), BF16 if later else F32)]
        + [jax.ShapeDtypeStruct((2 * count, wide), BF16)]
        + [jax.ShapeDtypeStruct((1, ds), F32)],
        scratch_shapes=[pltpu.VMEM((half, vocab), BF16)],
        compiler_params=pltpu.CompilerParams(vmem_limit_bytes=SMALL),
        cost_estimate=pl.CostEstimate(
            flops=2 * half * vocab * ds,
            bytes_accessed=2 * vocab * ds,
            transcendentals=2 * vocab * half,
        ),
    )(teacher, student, normed, rows, gain, held(own), held(other), *([before] if later else []))
    return out[:3], out[3], out[4], out[5], out[6]


def small(kernel, out_shape, *args):
    vmem = pl.BlockSpec(memory_space=pltpu.VMEM)
    return pl.pallas_call(
        kernel,
        in_specs=[vmem] * len(args),
        out_specs=[vmem] * len(out_shape),
        out_shape=[jax.ShapeDtypeStruct(*shape) for shape in out_shape],
        compiler_params=pltpu.CompilerParams(vmem_limit_bytes=SMALL),
    )(*args)


def added(kept, pieces, rows=slice(None)):
    first, second, third = (piece[rows].astype(F32) for piece in pieces)
    return (kept[...] + first) + (second + third)


def tail_rows(gain, count):
    high = gain.astype(BF16).astype(F32)
    low = gain - high
    wide = gain.shape[1] // 2
    rows = [p[:, n * wide : (n + 1) * wide] for n in range(2) for p in (high, low)]
    return jnp.concatenate(rows + [jnp.zeros((count - 4, wide), F32)], axis=0)


def tail_gain(piece, first):
    tail = piece[first : first + 16].astype(F32)
    return jnp.concatenate([tail[0:1] + tail[1:2], tail[2:3] + tail[3:4]], axis=1)


def between_a(*refs):
    kept_0, got_0, kept_1, got_1, gain = refs[0], refs[1:4], refs[4], refs[5:8], refs[8]
    kept, sends, gain_out = refs[9], refs[10:13], refs[13]
    rows = kept_0.shape[0]
    half = rows // 2
    first = added(kept_0, got_0)
    second = added(kept_1, got_1, slice(0, rows))
    gains = [tail_gain(piece, rows) for piece in got_1]
    total = (gain[...] + gains[0]) + (gains[1] + gains[2])
    gain_out[...] = total
    tail = tail_rows(total, 16)
    kept[...] = first[:half]
    for send, piece in zip(sends, (first[half:], second[:half], second[half:])):
        send[...] = jnp.concatenate([piece, tail], axis=0).astype(BF16)


def between_b(*refs):
    total = added(refs[0], refs[1:4])
    half = total.shape[0] // 2
    for s in range(4):
        piece = jnp.concatenate(
            [total[n * half + 16 * s : n * half + 16 * s + 16] for n in range(2)], axis=0
        )
        refs[4 + s][...] = piece.astype(refs[4 + s].dtype)


def before_z(*refs):
    kept_a, got_a, kept_b, got_b, gain = refs[0], refs[1:4], refs[4], refs[5:8], refs[8]
    kept, sends, gain_out = refs[9], refs[10:13], refs[13]
    rows = kept_a.shape[0]
    unit = rows // 4
    total = jnp.concatenate(
        [added(kept_a, got_a, slice(0, rows)), added(kept_b, got_b)], axis=1
    )
    gains = [tail_gain(piece, rows) for piece in got_a]
    share = (gain[...] + gains[0]) + (gains[1] + gains[2])
    gain_out[...] = share
    high = share.astype(BF16).astype(F32)
    tail = jnp.concatenate(
        [high, share - high, jnp.zeros((14 - unit, share.shape[1]), F32)], axis=0
    )
    kept[...] = total[:unit]
    for send, n in zip(sends, (2, 1, 3)):
        piece = total[n * unit : (n + 1) * unit]
        send[...] = jnp.concatenate([piece, tail], axis=0).astype(BF16)


def last_gain(kept, first, second, third, out):
    unit = first.shape[0] // 2
    tails = [piece[...].astype(F32)[unit:] for piece in (first, second, third)]
    shares = [tail[0:1] + tail[1:2] for tail in tails]
    out[...] = (kept[...] + shares[0]) + (shares[1] + shares[2])


def last_states(kept, first, second, third, states, gain, out):
    unit = kept.shape[0]
    pieces = [piece[...].astype(F32)[:unit] for piece in (first, second, third)]
    total = (kept[...] + pieces[0]) + (pieces[1] + pieces[2])
    own = states[...]
    inverse = lax.rsqrt(jnp.mean(own * own, axis=1, keepdims=True) + EPSILON)
    scaled = total * gain[...]
    out[...] = inverse * scaled - own * (inverse * inverse * inverse) * jnp.mean(
        own * scaled, axis=1, keepdims=True
    )


def body(hidden_states, final_gain, student_head, teacher_states, teacher_head, token_weight):
    y, zl, x, zh, c = (lax.axis_index(name) for name in AXES)
    z = zh * 2 + zl
    sign = 1 - 2 * c
    tokens = token_weight.shape[0]
    dt, ds = teacher_states.shape[1], hidden_states.shape[1]
    rows = hidden_states.shape[0] // 2
    unit = rows // 8
    half = tokens // 4

    def swap(array):
        return permute(array, lambda y, z, x, c: (y, z, x, 1 - c))

    kx, kz, i = row_parts(rows, 4, 2, unit)
    source = (((x + sign * kx) % 4 * 2 + (zh ^ kz)) * 2 + c) * unit + i
    select = pick(source, 2 * rows).astype(BF16)
    own = jnp.concatenate(
        [
            jnp.dot(select, states, preferred_element_type=F32).astype(BF16)
            for states in (teacher_states, hidden_states)
        ],
        axis=1,
    )
    teacher_other = swap(teacher_head)
    student_other = swap(student_head)

    from_y = moved(("y", "y"), -1)
    from_z = moved(("z", "z"), -1)
    own_states = own[:unit, dt:].astype(F32)
    y1, z0, own_states = lax.optimization_barrier(
        (permute(own, from_y), permute(own, from_z), own_states)
    )
    y2, z1 = lax.optimization_barrier((permute(y1, from_y), permute(y1, from_z)))
    gain_row = final_gain[None]
    y3, z2 = permute(y2, from_y), permute(y2, from_z)
    heads = (teacher_head, student_head, teacher_other, student_other)
    half_0 = logits_streamed([own, z0, y1, z1], gain_row, *heads)
    y3, z2, half_0, heads = lax.optimization_barrier((y3, z2, half_0, heads))
    z3_t, z3_h = permute(y3[:, :dt], from_z), permute(z2[:, dt:], from_y)
    student_heads = resident(heads[1], heads[3])
    z3_t, z3_h, student_heads = lax.optimization_barrier((z3_t, z3_h, student_heads))
    half_1 = logits(
        [y2, z2, y3, z3_t, z3_h],
        gain_row,
        *(heads[0], student_heads[0], heads[2], student_heads[1]),
    )

    ry, rb, kx, kz, i = row_parts(2 * half, 4, 2, 4, 2, unit)
    rz = kz * 2 + rb
    to_y, to_z, to_x = (y + sign * ry) % 4, (z + sign * rz) % 4, (x + sign * kx) % 4
    absolute = (((to_y * 2 + to_z % 2) * 4 + to_x) * 2 + to_z // 2) * unit + i
    order = pick(absolute, 2 * half).astype(F32)
    token = (absolute // unit * 2 + c) * unit + i
    weight = jnp.sum(jnp.where(pick(token, tokens), token_weight[None, :], 0.0), axis=1)

    local = jnp.concatenate([half_0[2][:2], half_1[2][:2]], axis=1)
    whole = jnp.dot(local, order, precision=lax.Precision.HIGHEST)
    spread = jnp.broadcast_to(whole.reshape(1, 8, -1), (64, 8, half // 2))
    every = lax.all_to_all(spread, AXES[:4], 0, 0, tiled=True)
    top = jnp.max(every, axis=0)
    whole = (top + jnp.log(jnp.sum(jnp.exp(every - top), axis=0))).reshape(whole.shape)
    relative = jnp.dot(whole, order.T, precision=lax.Precision.HIGHEST)
    rows = jnp.concatenate([relative, weight[None], jnp.zeros((5, 2 * half), F32)], axis=0)

    def exchange(pieces, axis):
        moves = {s: permute(pieces[s - 1], moved((axis, axis), s)) for s in (1, 3, 2)}
        return [moves[s] for s in (1, 2, 3)]

    head_pair = student_heads
    sends_0, kept_0, kept_b, send_b1, gain_0 = backward(
        half_0, rows[:, :half], gain_row, *head_pair
    )
    got_0 = exchange(sends_0, "x")
    got_b1 = permute(send_b1, moved(("y", "y"), 1))
    sends_1, kept_1, send_b2, send_b3, gain = backward(
        half_1, rows[:, half:], gain_row, *head_pair, gain_0
    )
    got_0, got_b1, sends_1, send_b2, send_b3 = lax.optimization_barrier(
        (got_0, got_b1, sends_1, send_b2, send_b3)
    )
    got_1 = exchange(sends_1, "x")
    got_b3 = permute(send_b3, moved(("y", "y"), 3))
    got_b2 = permute(send_b2, moved(("y", "y"), 2))
    wide = ds // 2
    count = half // 8
    kept_a, *sends_a, gain = small(
        between_a,
        [((count, wide), F32)] + [((count + 16, wide), BF16)] * 3 + [((1, ds), F32)],
        *(kept_0, *got_0, kept_1, *got_1, gain),
    )
    got_a = exchange(sends_a, "y")
    kept_b, *sends_b = small(
        between_b,
        [((count, wide), F32)] + [((count, wide), BF16)] * 3,
        *(kept_b, got_b1, got_b2, got_b3),
    )
    got_b = exchange(sends_b, "x")
    kept, *sends, gain = small(
        before_z,
        [((unit, ds), F32)] + [((16, ds), BF16)] * 3 + [((1, ds), F32)],
        *(kept_a, *got_a, kept_b, *got_b, gain),
    )
    got = exchange(sends, "z")
    (gain,) = small(last_gain, [((1, ds), F32)], gain, *got)
    gain_grad = (gain + swap(gain))[0]
    (states_grad,) = small(
        last_states, [((unit, ds), F32)], kept, *got, own_states, gain_row
    )
    return (states_grad, gain_grad)


def solution(mesh):
    torus = Mesh(mesh.devices.reshape(SIZES), AXES)
    return jax.shard_map(
        body,
        mesh=torus,
        in_specs=(
            P(("y", "zl"), None),
            P(),
            P(AXES, None),
            P(("y", "zl"), None),
            P(AXES, None),
            P(),
        ),
        out_specs=(P(AXES, None), P()),
        check_vma=False,
    )
```

profile of v0, /device:TPU:1, one launch (start us, length us, event | category | flops | bytes accessed | tf_op | source)
XLA Modules:
  0.0 183.8 jit_solution(2962399418505206900)
XLA Ops:
  0.6 1.5 collective-permute-start.6
  2.3 1.5 convolution_convert_fusion.1
  4.3 1.4 collective-permute-start
  5.7 1.6 collective-permute-start.1
  7.4 12.0 %collective-permute-done.refs_2_ = bf16[64,8192]{1,0:T(8,128)(2,1)S(1)} collective-permute-done((bf16[64,8192]{1,0:T(8,128)(2,1)S(1)}, bf16[64,8192]{1,0:T(8,128)(2,1)S(1)}, u32[]{:S(2)}, u32[]{:S(2)}) %collective-permute-start) | collective-permute-done | bytes 1048608 | tf_op jit(solution)/shard_map/ppermute | solution.py:33
  19.3 2.3 %collective-permute-done.1.refs_1_ = bf16[64,8192]{1,0:T(8,128)(2,1)S(1)} collective-permute-done((bf16[64,8192]{1,0:T(8,128)(2,1)S(1)}, bf16[64,8192]{1,0:T(8,128)(2,1)S(1)}, u32[]{:S(2)}, u32[]{:S(2)}) %collective-permute-start.1) | collective-permute-done | bytes 1048608 | tf_op jit(solution)/shard_map/ppermute | solution.py:33
  23.0 13.6 %collective-permute-done.2.refs_0_ = bf16[64,8192]{1,0:T(8,128)(2,1)S(1)} collective-permute-done((bf16[64,8192]{1,0:T(8,128)(2,1)S(1)}, bf16[64,8192]{1,0:T(8,128)(2,1)S(1)}, u32[]{:S(2)}, u32[]{:S(2)}) %collective-permute-start.2) | collective-permute-done | bytes 1048608 | tf_op jit(solution)/shard_map/ppermute | solution.py:33
  40.0 17.1 %shard_map.77 = (f32[256,2048]{1,0:T(8,128)}, f32[256,2048]{1,0:T(8,128)}, f32[8,256]{1,0:T(8,128)}, bf16[256,3584]{1,0:T(8,128)(2,1)}) custom-call(bf16[64,8192]{1,0:T(8,128)(2,1)} %copy-done.18, bf16[64,8192]{1,0:T(8,128)(2,1)} %copy-done.20, bf16[64,8192]{1,0:T(8,128)(2,1)} %copy-done.19, bf16[64,8192]{1,0:T(8,128)(2,1)} %copy-done.21, ...), custom_call_target="tpu_custom_call" | custom-call | flops 8589934592 | bytes 33554432 | tf_op jit(solution)/shard_map/pallas_call | solution.py:219
  60.1 5.2 %shard_map.78 = (bf16[1024,3584]{1,0:T(8,128)(2,1)S(1)}, bf16[1024,3584]{1,0:T(8,128)(2,1)S(1)}) custom-call(bf16[1024,3584]{1,0:T(8,128)(2,1)} %refs_0_, bf16[1024,3584]{1,0:T(8,128)(2,1)} %collective-permute-done.7.refs_8_.refs_1_), custom_call_target="tpu_custom_call" | custom-call | bytes 29360128 | tf_op jit(solution)/shard_map/pallas_call | solution.py:84
  65.3 2.8 %collective-permute-done.9.refs_4_ = bf16[64,3584]{1,0:T(8,128)(2,1)} collective-permute-done((bf16[64,3584]{1,0:T(8,128)(2,1)}, bf16[64,3584]{1,0:T(8,128)(2,1)}, u32[]{:S(2)}, u32[]{:S(2)}) %collective-permute-start.9) | collective-permute-done | bytes 458784 | tf_op jit(solution)/shard_map/ppermute | solution.py:33
  68.2 13.6 %shard_map.79 = (f32[256,2048]{1,0:T(8,128)S(1)}, f32[256,2048]{1,0:T(8,128)S(1)}, f32[8,256]{1,0:T(8,128)S(1)}, bf16[256,3584]{1,0:T(8,128)(2,1)S(1)}) custom-call(bf16[64,8192]{1,0:T(8,128)(2,1)S(1)} %collective-permute-done.2.refs_0_, bf16[64,8192]{1,0:T(8,128)(2,1)S(1)} %collective-permute-done.5.refs_1_, ...), custom_call_target="tpu_custom_call" | custom-call | flops 8589934592 | bytes 33554432 | tf_op jit(solution)/shard_map/pallas_call | solution.py:255
  83.1 1.3 copy-done.12
  87.0 9.1 %all-to-all-start = ((f32[64,8,128]{2,1,0:T(8,128)}), f32[64,8,128]{2,1,0:T(8,128)S(1)}, u32[]{:S(2)}, u32[]{:S(2)}) async-start(f32[64,8,128]{2,1,0:T(8,128)} %broadcast_in_dim.35), calls=%async_computation | async-start | bytes 524288 | tf_op jit(solution)/shard_map/all_to_all | solution.py:510
  96.5 8.9 %all-to-all-done = f32[64,8,128]{2,1,0:T(8,128)S(1)} async-done(((f32[64,8,128]{2,1,0:T(8,128)}), f32[64,8,128]{2,1,0:T(8,128)S(1)}, u32[]{:S(2)}, u32[]{:S(2)}) %all-to-all-start) | async-done | bytes 262176 | tf_op jit(solution)/shard_map/all_to_all | solution.py:510
  106.3 3.1 %copy-done.3 = bf16[1024,3584]{1,0:T(8,128)(2,1)S(1)} copy-done((bf16[1024,3584]{1,0:T(8,128)(2,1)S(1)}, bf16[1024,3584]{1,0:T(8,128)(2,1)}, u32[]{:S(2)}) %copy-start.3) | copy-done | bytes 7340056
  109.4 3.1 %copy-done.6 = bf16[1024,3584]{1,0:T(8,128)(2,1)S(1)} copy-done((bf16[1024,3584]{1,0:T(8,128)(2,1)S(1)}, bf16[1024,3584]{1,0:T(8,128)(2,1)}, u32[]{:S(2)}) %copy-start.6) | copy-done | bytes 7340056
  112.5 1.6 copy-done.8
  114.1 1.6 copy-done.9
  115.7 5.2 %shard_map.80 = (bf16[64,1792]{1,0:T(8,128)(2,1)S(1)}, bf16[64,1792]{1,0:T(8,128)(2,1)S(1)}, bf16[64,1792]{1,0:T(8,128)(2,1)S(1)}, f32[64,1792]{1,0:T(8,128)S(1)...) custom-call(f32[256,2048]{1,0:T(8,128)S(1)} %copy-done.8, ...), custom_call_target="tpu_custom_call" | custom-call | flops 3758096384 | bytes 14680064 | tf_op jit(solution)/shard_map/pallas_call | solution.py:337
  122.4 1.5 collective-permute-start.11
  123.9 5.2 %shard_map.81 = (bf16[80,1792]{1,0:T(8,128)(2,1)S(1)}, bf16[80,1792]{1,0:T(8,128)(2,1)S(1)}, bf16[80,1792]{1,0:T(8,128)(2,1)S(1)}, f32[64,1792]{1,0:T(8,128)S(1)...) custom-call(f32[256,2048]{1,0:T(8,128)S(1)} %copy-done.11, ...), custom_call_target="tpu_custom_call" | custom-call | flops 3758096384 | bytes 14680064 | tf_op jit(solution)/shard_map/pallas_call | solution.py:337
  129.1 2.1 %collective-permute-done.12.refs_3_ = bf16[64,1792]{1,0:T(8,128)(2,1)S(1)} collective-permute-done((bf16[64,1792]{1,0:T(8,128)(2,1)S(1)}, bf16[64,1792]{1,0:T(8,128)(2,1)S(1)}, u32[]{:S(2)}, u32[]{:S(2)}) %collective-permute-start.12) | collective-permute-done | bytes 229408 | tf_op jit(solution)/shard_map/ppermute | solution.py:33
  133.3 1.7 collective-permute-start.15
  135.6 6.1 %collective-permute-done.14.refs_5_ = bf16[80,1792]{1,0:T(8,128)(2,1)S(1)} collective-permute-done((bf16[80,1792]{1,0:T(8,128)(2,1)S(1)}, bf16[80,1792]{1,0:T(8,128)(2,1)S(1)}, u32[]{:S(2)}, u32[]{:S(2)}) %collective-permute-start.14) | collective-permute-done | bytes 286752 | tf_op jit(solution)/shard_map/ppermute | solution.py:33
  141.7 2.2 %collective-permute-done.16.refs_7_ = bf16[80,1792]{1,0:T(8,128)(2,1)S(1)} collective-permute-done((bf16[80,1792]{1,0:T(8,128)(2,1)S(1)}, bf16[80,1792]{1,0:T(8,128)(2,1)S(1)}, u32[]{:S(2)}, u32[]{:S(2)}) %collective-permute-start.16) | collective-permute-done | bytes 286752 | tf_op jit(solution)/shard_map/ppermute | solution.py:33
  144.2 2.4 %collective-permute-start.17 = (bf16[48,1792]{1,0:T(8,128)(2,1)S(1)}, bf16[48,1792]{1,0:T(8,128)(2,1)S(1)}, u32[]{:S(2)}, u32[]{:S(2)}) collective-permute-start(bf16[48,1792]{1,0:T(8,128)(2,1)S(1)} %get-tuple-element.116), channel_id=1, source_target_pairs={{0,32},{1,97},{4,36},{5,101},{8,40},{9,105},{12,44},{13,109},{16,4... | collective-permute-start | bytes 516104 | tf_op jit(solution)/shard_map/ppermute | solution.py:33
  147.5 3.3 %collective-permute-start.22 = (bf16[32,1792]{1,0:T(8,128)(2,1)S(1)}, bf16[32,1792]{1,0:T(8,128)(2,1)S(1)}, u32[]{:S(2)}, u32[]{:S(2)}) collective-permute-start(bf16[32,1792]{1,0:T(8,128)(2,1)S(1)} %get-tuple-element.124), channel_id=1, source_target_pairs={{0,4},{1,13},{4,8},{5,1},{8,12},{9,5},{12,0},{13,9},{16,20},{17,29... | collective-permute-start | bytes 344072 | tf_op jit(solution)/shard_map/ppermute | solution.py:33
  150.8 5.5 %collective-permute-done.17.refs_1_ = bf16[48,1792]{1,0:T(8,128)(2,1)S(1)} collective-permute-done((bf16[48,1792]{1,0:T(8,128)(2,1)S(1)}, bf16[48,1792]{1,0:T(8,128)(2,1)S(1)}, u32[]{:S(2)}, u32[]{:S(2)}) %collective-permute-start.17) | collective-permute-done | bytes 172064 | tf_op jit(solution)/shard_map/ppermute | solution.py:33
  157.1 4.1 %collective-permute-done.24.refs_7_ = bf16[32,1792]{1,0:T(8,128)(2,1)S(1)} collective-permute-done((bf16[32,1792]{1,0:T(8,128)(2,1)S(1)}, bf16[32,1792]{1,0:T(8,128)(2,1)S(1)}, u32[]{:S(2)}, u32[]{:S(2)}) %collective-permute-start.24) | collective-permute-done | bytes 114720 | tf_op jit(solution)/shard_map/ppermute | solution.py:33
  163.4 2.1 %collective-permute-done.25.first = bf16[16,3584]{1,0:T(8,128)(2,1)S(1)} collective-permute-done((bf16[16,3584]{1,0:T(8,128)(2,1)S(1)}, bf16[16,3584]{1,0:T(8,128)(2,1)S(1)}, u32[]{:S(2)}, u32[]{:S(2)}) %collective-permute-start.25) | collective-permute-done | bytes 114720 | tf_op jit(solution)/shard_map/ppermute | solution.py:33
  165.4 2.6 %collective-permute-done.26.second = bf16[16,3584]{1,0:T(8,128)(2,1)S(1)} collective-permute-done((bf16[16,3584]{1,0:T(8,128)(2,1)S(1)}, bf16[16,3584]{1,0:T(8,128)(2,1)S(1)}, u32[]{:S(2)}, u32[]{:S(2)}) %collective-permute-start.26) | collective-permute-done | bytes 114720 | tf_op jit(solution)/shard_map/ppermute | solution.py:33
  169.3 12.7 %collective-permute-start.28 = (f32[1,3584]{1,0:T(1,128)S(1)}, f32[1,3584]{1,0:T(1,128)S(1)}, u32[]{:S(2)}, u32[]{:S(2)}) collective-permute-start(f32[1,3584]{1,0:T(1,128)S(1)} %shard_map.86), channel_id=1, source_target_pairs={{0,1},{1,0},{4,5},{5,4},{8,9},{9,8},{12,13},{13,12},{16,17},{17,16... | collective-permute-start | bytes 43016 | tf_op jit(solution)/shard_map/ppermute | solution.py:33
  (111 shorter events, 24.7 us)
Async XLA Ops:
  0.6 39.3 %collective-permute-start.6 = (bf16[1024,4608]{1,0:T(8,128)(2,1)}, bf16[1024,4608]{1,0:T(8,128)(2,1)}, u32[]{:S(2)}, u32[]{:S(2)}) collective-permute-start(bf16[1024,4608]{1,0:T(8,128)(2,1)} %refs_6_.2), channel_id=1, source_target_pairs={{0,1},{1,0},{4,5},{5,4},{8,9},{9,8},{12,13},{13,12},{16,17},{17,16... | collective-permute-start | bytes 28311560 | tf_op jit(solution)/shard_map/ppermute | solution.py:33
  2.1 37.8 %collective-permute-start.7 = (bf16[1024,3584]{1,0:T(8,128)(2,1)}, bf16[1024,3584]{1,0:T(8,128)(2,1)}, u32[]{:S(2)}, u32[]{:S(2)}) collective-permute-start(bf16[1024,3584]{1,0:T(8,128)(2,1)} %refs_0_), channel_id=1, source_target_pairs={{0,1},{1,0},{4,5},{5,4},{8,9},{9,8},{12,13},{13,12},{16,17},{17,16... | collective-permute-start | bytes 22020104 | tf_op jit(solution)/shard_map/ppermute | solution.py:33
  4.3 35.7 %copy-start.18 = (bf16[64,8192]{1,0:T(8,128)(2,1)}, bf16[64,8192]{1,0:T(8,128)(2,1)S(1)}, u32[]{:S(2)}) copy-start(bf16[64,8192]{1,0:T(8,128)(2,1)S(1)} %pad_maximum_fusion.refs_0_) | copy-start | bytes 3145732
  4.3 15.1 %collective-permute-start = (bf16[64,8192]{1,0:T(8,128)(2,1)S(1)}, bf16[64,8192]{1,0:T(8,128)(2,1)S(1)}, u32[]{:S(2)}, u32[]{:S(2)}) collective-permute-start(bf16[64,8192]{1,0:T(8,128)(2,1)S(1)} %pad_maximum_fusion.refs_0_), channel_id=1, source_target_pairs={{0,96},{1,33},{4,100},{5,37},{8,104},{9,41},{12,108},{13,45},{16,1... | collective-permute-start | bytes 3145736 | tf_op jit(solution)/shard_map/ppermute | solution.py:33
  5.7 15.9 %collective-permute-start.1 = (bf16[64,8192]{1,0:T(8,128)(2,1)S(1)}, bf16[64,8192]{1,0:T(8,128)(2,1)S(1)}, u32[]{:S(2)}, u32[]{:S(2)}) collective-permute-start(bf16[64,8192]{1,0:T(8,128)(2,1)S(1)} %pad_maximum_fusion.refs_0_), channel_id=1, source_target_pairs={{0,18},{1,17},{4,22},{5,21},{8,26},{9,25},{12,30},{13,29},{16,0},{... | collective-permute-start | bytes 3145736 | tf_op jit(solution)/shard_map/ppermute | solution.py:33
  21.7 14.9 %collective-permute-start.2 = (bf16[64,8192]{1,0:T(8,128)(2,1)S(1)}, bf16[64,8192]{1,0:T(8,128)(2,1)S(1)}, u32[]{:S(2)}, u32[]{:S(2)}) collective-permute-start(bf16[64,8192]{1,0:T(8,128)(2,1)S(1)} %collective-permute-done.refs_2_), channel_id=1, source_target_pairs={{0,96},{1,33},{4,100},{5,37},{8,104},{9,41},{12,108},{13,45},{16,1... | collective-permute-start | bytes 3145736 | tf_op jit(solution)/shard_map/ppermute | solution.py:33
  23.0 14.9 %collective-permute-start.3 = (bf16[64,8192]{1,0:T(8,128)(2,1)S(1)}, bf16[64,8192]{1,0:T(8,128)(2,1)S(1)}, u32[]{:S(2)}, u32[]{:S(2)}) collective-permute-start(bf16[64,8192]{1,0:T(8,128)(2,1)S(1)} %collective-permute-done.refs_2_), channel_id=1, source_target_pairs={{0,18},{1,17},{4,22},{5,21},{8,26},{9,25},{12,30},{13,29},{16,0},{... | collective-permute-start | bytes 3145736 | tf_op jit(solution)/shard_map/ppermute | solution.py:33
  37.8 19.3 %collective-permute-start.4 = (bf16[64,8192]{1,0:T(8,128)(2,1)S(1)}, bf16[64,8192]{1,0:T(8,128)(2,1)S(1)}, u32[]{:S(2)}, u32[]{:S(2)}) collective-permute-start(bf16[64,8192]{1,0:T(8,128)(2,1)S(1)} %collective-permute-done.2.refs_0_), channel_id=1, source_target_pairs={{0,96},{1,33},{4,100},{5,37},{8,104},{9,41},{12,108},{13,45},{16,1... | collective-permute-start | bytes 3145736 | tf_op jit(solution)/shard_map/ppermute | solution.py:33
  38.8 18.3 %collective-permute-start.5 = (bf16[64,8192]{1,0:T(8,128)(2,1)S(1)}, bf16[64,8192]{1,0:T(8,128)(2,1)S(1)}, u32[]{:S(2)}, u32[]{:S(2)}) collective-permute-start(bf16[64,8192]{1,0:T(8,128)(2,1)S(1)} %collective-permute-done.2.refs_0_), channel_id=1, source_target_pairs={{0,18},{1,17},{4,22},{5,21},{8,26},{9,25},{12,30},{13,29},{16,0},{... | collective-permute-start | bytes 3145736 | tf_op jit(solution)/shard_map/ppermute | solution.py:33
  57.9 10.3 %collective-permute-start.8 = (bf16[64,4608]{1,0:T(8,128)(2,1)}, bf16[64,4608]{1,0:T(8,128)(2,1)}, u32[]{:S(2)}, u32[]{:S(2)}) collective-permute-start(bf16[64,4608]{1,0:T(8,128)(2,1)} %slice.23), channel_id=1, source_target_pairs={{0,18},{1,17},{4,22},{5,21},{8,26},{9,25},{12,30},{13,29},{16,0},{... | collective-permute-start | bytes 1769480 | tf_op jit(solution)/shard_map/ppermute | solution.py:33
  59.1 9.0 %collective-permute-start.9 = (bf16[64,3584]{1,0:T(8,128)(2,1)}, bf16[64,3584]{1,0:T(8,128)(2,1)}, u32[]{:S(2)}, u32[]{:S(2)}) collective-permute-start(bf16[64,3584]{1,0:T(8,128)(2,1)} %slice.24), channel_id=1, source_target_pairs={{0,96},{1,33},{4,100},{5,37},{8,104},{9,41},{12,108},{13,45},{16,1... | collective-permute-start | bytes 1376264 | tf_op jit(solution)/shard_map/ppermute | solution.py:33
  87.0 18.4 %all-to-all-start = ((f32[64,8,128]{2,1,0:T(8,128)}), f32[64,8,128]{2,1,0:T(8,128)S(1)}, u32[]{:S(2)}, u32[]{:S(2)}) async-start(f32[64,8,128]{2,1,0:T(8,128)} %broadcast_in_dim.35), calls=%async_computation | async-start | bytes 524288 | tf_op jit(solution)/shard_map/all_to_all | solution.py:510
  120.9 10.3 %collective-permute-start.13 = (bf16[128,1792]{1,0:T(8,128)(2,1)S(1)}, bf16[128,1792]{1,0:T(8,128)(2,1)S(1)}, u32[]{:S(2)}, u32[]{:S(2)}) collective-permute-start(bf16[128,1792]{1,0:T(8,128)(2,1)S(1)} %get-tuple-element.97), channel_id=1, source_target_pairs={{0,32},{1,97},{4,36},{5,101},{8,40},{9,105},{12,44},{13,109},{16,4... | collective-permute-start | bytes 1376264 | tf_op jit(solution)/shard_map/ppermute | solution.py:33
  121.7 7.4 %collective-permute-start.10 = (bf16[64,1792]{1,0:T(8,128)(2,1)S(1)}, bf16[64,1792]{1,0:T(8,128)(2,1)S(1)}, u32[]{:S(2)}, u32[]{:S(2)}) collective-permute-start(bf16[64,1792]{1,0:T(8,128)(2,1)S(1)} %get-tuple-element.94), channel_id=1, source_target_pairs={{0,4},{1,13},{4,8},{5,1},{8,12},{9,5},{12,0},{13,9},{16,20},{17,29... | collective-permute-start | bytes 688136 | tf_op jit(solution)/shard_map/ppermute | solution.py:33
  122.4 6.7 %collective-permute-start.11 = (bf16[64,1792]{1,0:T(8,128)(2,1)S(1)}, bf16[64,1792]{1,0:T(8,128)(2,1)S(1)}, u32[]{:S(2)}, u32[]{:S(2)}) collective-permute-start(bf16[64,1792]{1,0:T(8,128)(2,1)S(1)} %get-tuple-element.95), channel_id=1, source_target_pairs={{0,8},{1,9},{4,12},{5,13},{8,0},{9,1},{12,4},{13,5},{16,24},{17,25... | collective-permute-start | bytes 688136 | tf_op jit(solution)/shard_map/ppermute | solution.py:33
  123.9 7.4 %collective-permute-start.12 = (bf16[64,1792]{1,0:T(8,128)(2,1)S(1)}, bf16[64,1792]{1,0:T(8,128)(2,1)S(1)}, u32[]{:S(2)}, u32[]{:S(2)}) collective-permute-start(bf16[64,1792]{1,0:T(8,128)(2,1)S(1)} %get-tuple-element.96), channel_id=1, source_target_pairs={{0,12},{1,5},{4,0},{5,9},{8,4},{9,13},{12,8},{13,1},{16,28},{17,21... | collective-permute-start | bytes 688136 | tf_op jit(solution)/shard_map/ppermute | solution.py:33
  131.2 16.0 %collective-permute-start.20 = (bf16[128,1792]{1,0:T(8,128)(2,1)S(1)}, bf16[128,1792]{1,0:T(8,128)(2,1)S(1)}, u32[]{:S(2)}, u32[]{:S(2)}) collective-permute-start(bf16[128,1792]{1,0:T(8,128)(2,1)S(1)} %get-tuple-element.121), channel_id=1, source_target_pairs={{0,64},{1,65},{4,68},{5,69},{8,72},{9,73},{12,76},{13,77},{16,80},... | collective-permute-start | bytes 1376264 | tf_op jit(solution)/shard_map/ppermute | solution.py:33
  132.4 9.4 %collective-permute-start.14 = (bf16[80,1792]{1,0:T(8,128)(2,1)S(1)}, bf16[80,1792]{1,0:T(8,128)(2,1)S(1)}, u32[]{:S(2)}, u32[]{:S(2)}) collective-permute-start(bf16[80,1792]{1,0:T(8,128)(2,1)S(1)} %get-tuple-element.111), channel_id=1, source_target_pairs={{0,4},{1,13},{4,8},{5,1},{8,12},{9,5},{12,0},{13,9},{16,20},{17,29... | collective-permute-start | bytes 860168 | tf_op jit(solution)/shard_map/ppermute | solution.py:33
  133.3 8.4 %collective-permute-start.15 = (bf16[80,1792]{1,0:T(8,128)(2,1)S(1)}, bf16[80,1792]{1,0:T(8,128)(2,1)S(1)}, u32[]{:S(2)}, u32[]{:S(2)}) collective-permute-start(bf16[80,1792]{1,0:T(8,128)(2,1)S(1)} %get-tuple-element.112), channel_id=1, source_target_pairs={{0,8},{1,9},{4,12},{5,13},{8,0},{9,1},{12,4},{13,5},{16,24},{17,25... | collective-permute-start | bytes 860168 | tf_op jit(solution)/shard_map/ppermute | solution.py:33
  135.0 9.0 %collective-permute-start.16 = (bf16[80,1792]{1,0:T(8,128)(2,1)S(1)}, bf16[80,1792]{1,0:T(8,128)(2,1)S(1)}, u32[]{:S(2)}, u32[]{:S(2)}) collective-permute-start(bf16[80,1792]{1,0:T(8,128)(2,1)S(1)} %get-tuple-element.113), channel_id=1, source_target_pairs={{0,12},{1,5},{4,0},{5,9},{8,4},{9,13},{12,8},{13,1},{16,28},{17,21... | collective-permute-start | bytes 860168 | tf_op jit(solution)/shard_map/ppermute | solution.py:33
  135.2 12.1 %collective-permute-start.21 = (bf16[128,1792]{1,0:T(8,128)(2,1)S(1)}, bf16[128,1792]{1,0:T(8,128)(2,1)S(1)}, u32[]{:S(2)}, u32[]{:S(2)}) collective-permute-start(bf16[128,1792]{1,0:T(8,128)(2,1)S(1)} %get-tuple-element.122), channel_id=1, source_target_pairs={{0,96},{1,33},{4,100},{5,37},{8,104},{9,41},{12,108},{13,45},{16,1... | collective-permute-start | bytes 1376264 | tf_op jit(solution)/shard_map/ppermute | solution.py:33
  144.2 12.1 %collective-permute-start.17 = (bf16[48,1792]{1,0:T(8,128)(2,1)S(1)}, bf16[48,1792]{1,0:T(8,128)(2,1)S(1)}, u32[]{:S(2)}, u32[]{:S(2)}) collective-permute-start(bf16[48,1792]{1,0:T(8,128)(2,1)S(1)} %get-tuple-element.116), channel_id=1, source_target_pairs={{0,32},{1,97},{4,36},{5,101},{8,40},{9,105},{12,44},{13,109},{16,4... | collective-permute-start | bytes 516104 | tf_op jit(solution)/shard_map/ppermute | solution.py:33
  146.6 9.8 %collective-permute-start.18 = (bf16[48,1792]{1,0:T(8,128)(2,1)S(1)}, bf16[48,1792]{1,0:T(8,128)(2,1)S(1)}, u32[]{:S(2)}, u32[]{:S(2)}) collective-permute-start(bf16[48,1792]{1,0:T(8,128)(2,1)S(1)} %get-tuple-element.117), channel_id=1, source_target_pairs={{0,64},{1,65},{4,68},{5,69},{8,72},{9,73},{12,76},{13,77},{16,80},... | collective-permute-start | bytes 516104 | tf_op jit(solution)/shard_map/ppermute | solution.py:33
  146.6 10.0 %collective-permute-start.19 = (bf16[48,1792]{1,0:T(8,128)(2,1)S(1)}, bf16[48,1792]{1,0:T(8,128)(2,1)S(1)}, u32[]{:S(2)}, u32[]{:S(2)}) collective-permute-start(bf16[48,1792]{1,0:T(8,128)(2,1)S(1)} %get-tuple-element.118), channel_id=1, source_target_pairs={{0,96},{1,33},{4,100},{5,37},{8,104},{9,41},{12,108},{13,45},{16,1... | collective-permute-start | bytes 516104 | tf_op jit(solution)/shard_map/ppermute | solution.py:33
  147.3 36.2 %copy-start.1 = (bf16[128,4608]{1,0:T(8,128)(2,1)S(1)}, bf16[128,4608]{1,0:T(8,128)(2,1)}, u32[]{:S(2)}) copy-start(bf16[128,4608]{1,0:T(8,128)(2,1)} %param.9) | copy-start | bytes 3538948
  147.5 9.6 %collective-permute-start.22 = (bf16[32,1792]{1,0:T(8,128)(2,1)S(1)}, bf16[32,1792]{1,0:T(8,128)(2,1)S(1)}, u32[]{:S(2)}, u32[]{:S(2)}) collective-permute-start(bf16[32,1792]{1,0:T(8,128)(2,1)S(1)} %get-tuple-element.124), channel_id=1, source_target_pairs={{0,4},{1,13},{4,8},{5,1},{8,12},{9,5},{12,0},{13,9},{16,20},{17,29... | collective-permute-start | bytes 344072 | tf_op jit(solution)/shard_map/ppermute | solution.py:33
  150.8 6.3 %collective-permute-start.23 = (bf16[32,1792]{1,0:T(8,128)(2,1)S(1)}, bf16[32,1792]{1,0:T(8,128)(2,1)S(1)}, u32[]{:S(2)}, u32[]{:S(2)}) collective-permute-start(bf16[32,1792]{1,0:T(8,128)(2,1)S(1)} %get-tuple-element.125), channel_id=1, source_target_pairs={{0,8},{1,9},{4,12},{5,13},{8,0},{9,1},{12,4},{13,5},{16,24},{17,25... | collective-permute-start | bytes 344072 | tf_op jit(solution)/shard_map/ppermute | solution.py:33
  156.4 4.9 %collective-permute-start.24 = (bf16[32,1792]{1,0:T(8,128)(2,1)S(1)}, bf16[32,1792]{1,0:T(8,128)(2,1)S(1)}, u32[]{:S(2)}, u32[]{:S(2)}) collective-permute-start(bf16[32,1792]{1,0:T(8,128)(2,1)S(1)} %get-tuple-element.126), channel_id=1, source_target_pairs={{0,12},{1,5},{4,0},{5,9},{8,4},{9,13},{12,8},{13,1},{16,28},{17,21... | collective-permute-start | bytes 344072 | tf_op jit(solution)/shard_map/ppermute | solution.py:33
  161.4 4.0 %collective-permute-start.25 = (bf16[16,3584]{1,0:T(8,128)(2,1)S(1)}, bf16[16,3584]{1,0:T(8,128)(2,1)S(1)}, u32[]{:S(2)}, u32[]{:S(2)}) collective-permute-start(bf16[16,3584]{1,0:T(8,128)(2,1)S(1)} %get-tuple-element.129), channel_id=1, source_target_pairs={{0,16},{1,19},{4,20},{5,23},{8,24},{9,27},{12,28},{13,31},{16,2},{... | collective-permute-start | bytes 344072 | tf_op jit(solution)/shard_map/ppermute | solution.py:33
  162.6 5.4 %collective-permute-start.26 = (bf16[16,3584]{1,0:T(8,128)(2,1)S(1)}, bf16[16,3584]{1,0:T(8,128)(2,1)S(1)}, u32[]{:S(2)}, u32[]{:S(2)}) collective-permute-start(bf16[16,3584]{1,0:T(8,128)(2,1)S(1)} %get-tuple-element.130), channel_id=1, source_target_pairs={{0,2},{1,3},{4,6},{5,7},{8,10},{9,11},{12,14},{13,15},{16,18},{17,... | collective-permute-start | bytes 344072 | tf_op jit(solution)/shard_map/ppermute | solution.py:33
  162.9 6.4 %collective-permute-start.27 = (bf16[16,3584]{1,0:T(8,128)(2,1)S(1)}, bf16[16,3584]{1,0:T(8,128)(2,1)S(1)}, u32[]{:S(2)}, u32[]{:S(2)}) collective-permute-start(bf16[16,3584]{1,0:T(8,128)(2,1)S(1)} %get-tuple-element.131), channel_id=1, source_target_pairs={{0,18},{1,17},{4,22},{5,21},{8,26},{9,25},{12,30},{13,29},{16,0},{... | collective-permute-start | bytes 344072 | tf_op jit(solution)/shard_map/ppermute | solution.py:33
  169.3 13.5 %collective-permute-start.28 = (f32[1,3584]{1,0:T(1,128)S(1)}, f32[1,3584]{1,0:T(1,128)S(1)}, u32[]{:S(2)}, u32[]{:S(2)}) collective-permute-start(f32[1,3584]{1,0:T(1,128)S(1)} %shard_map.86), channel_id=1, source_target_pairs={{0,1},{1,0},{4,5},{5,4},{8,9},{9,8},{12,13},{13,12},{16,17},{17,16... | collective-permute-start | bytes 43016 | tf_op jit(solution)/shard_map/ppermute | solution.py:33
  (22 other events, 216.7 us)
where the time goes:
time: 187 us; the launch traced here: 184 us
  waiting for transfers between devices  67.8 us (36%)
  Pallas kernels  47.7 us (26%)
  starting transfers between devices  45.5 us (24%)
  local copies, waits for them, and re-layouts  17.2 us (9%)
  matrix products  3 us (2%)
    ppermute x29, waiting for transfers between devices, permute(): return lax.ppermute(array, AXES, pairs)  58.8 us
    ppermute x29, starting transfers between devices, permute(): return lax.ppermute(array, AXES, pairs)  36.4 us
    pallas_call x1, Pallas kernels, logits_streamed(): pl.pallas_call(functools.partial(streamed_kernel, tile), in_specs=[vmem]...  17.1 us
    pallas_call x1, Pallas kernels, logits(): pl.pallas_call(functools.partial(logits_kernel, tile), in_specs=[vmem] *...  13.6 us
    unnamed x48, local copies, waits for them, and re-layouts  13.4 us
    pallas_call x2, Pallas kernels, backward(): pl.pallas_call(functools.partial(backward_kernel, tile, later), in_specs=...  10.4 us
    all_to_all x1, starting transfers between devices, body(): every = lax.all_to_all(spread, AXES[:4], 0, 0, tiled=True)  9.06 us
    all_to_all x1, waiting for transfers between devices, body(): every = lax.all_to_all(spread, AXES[:4], 0, 0, tiled=True)  8.93 us
  transfers between devices with their start and end apart: 30, of which 17 were waited for; matrix products, arithmetic and copies ran while one was open for 2% of the time, Pallas kernels for 16%

commit v1 on v0

--- a/solution.py
+++ b/solution.py
@@ -15,6 +15,7 @@
 STREAMED = 58 * 2**20
 LARGE = 30 * 2**20
 SMALL = 3 * 2**20
+GAIN = (32, 128)
 
 
 def place(y, z, x, c):
@@ -53,6 +54,11 @@
         digits.append(index % size)
         index = index // size
     return digits[::-1]
+
+
+def log_sum(parts):
+    top = jnp.maximum(jnp.maximum(parts[0], parts[1]), jnp.maximum(parts[2], parts[3]))
+    return top + jnp.log(sum(jnp.exp(part - top) for part in parts))
 
 
 def columns_to_rows(columns):
@@ -297,7 +303,10 @@
         out += jnp.dot(grad[:, part:], other[:, at], preferred_element_type=F32)
         share = jnp.sum(out * normed[:, at].astype(F32), axis=0, keepdims=True)
         share /= gain[:, at]
-        gain_out[:, at] = share + before[:, at] if later else share
+        for n in range(tile // 128):
+            row = pl.ds(k * tile // 128 + n, 1)
+            piece = share[:, 128 * n : 128 * (n + 1)]
+            gain_out[row, :] = piece + before[row, :] if later else piece
         second = k >= steps // 2
         at = pl.ds((k - second * (steps // 2)) * tile, tile)
         if second:
@@ -314,15 +323,31 @@
                 if s == 0:
                     kept_a[:, at] = piece
                 else:
-                    sends_a[s - 1][pl.ds(0, half // 4), at] = piece.astype(BF16)
+                    sends_a[s - 1][:, at] = piece.astype(BF16)
+    used = ds // 128
+    gain_out[used:, :] = jnp.zeros((gain_out.shape[0] - used, 128), F32)
     if later:
-        share = gain_out[...]
-        high = share.astype(BF16).astype(F32)
-        low = share - high
-        tail = [p[:, n * ds // 2 : (n + 1) * ds // 2] for n in range(2) for p in (high, low)]
-        tail = jnp.concatenate(tail + [jnp.zeros((12, ds // 2), F32)], axis=0).astype(BF16)
+        tail = packed(gain_out[...], half // 4).astype(BF16)
         for send in sends_a:
-            send[pl.ds(half // 4, 16), :] = tail
+            send[:, pl.ds(ds // 2, 128)] = tail
+
+
+def packed(gain, rows):
+    high = gain.astype(BF16).astype(F32)
+    parts = jnp.concatenate([high, gain - high], axis=0)
+    count = parts.shape[0]
+    return jnp.concatenate(
+        [parts[first : first + rows] for first in range(0, count, rows)], axis=1
+    )
+
+
+def unpacked(tail):
+    tail = tail.astype(F32)
+    parts = jnp.concatenate(
+        [tail[:, first : first + 128] for first in range(0, tail.shape[1], 128)], axis=0
+    )
+    half = parts.shape[0] // 2
+    return parts[:half] + parts[half:]
 
 
 def backward(part_of, rows, gain, own, other, before=None):
@@ -338,11 +363,11 @@
         functools.partial(backward_kernel, tile, later),
         in_specs=[vmem] * (7 + later),
         out_specs=[vmem] * 7,
-        out_shape=[jax.ShapeDtypeStruct((count + 16 * later, wide), BF16)] * 3
+        out_shape=[jax.ShapeDtypeStruct((count, wide + 128 * later), BF16)] * 3
         + [jax.ShapeDtypeStruct((count, wide), F32)]
         + [jax.ShapeDtypeStruct((2 * count, wide), BF16 if later else F32)]
         + [jax.ShapeDtypeStruct((2 * count, wide), BF16)]
-        + [jax.ShapeDtypeStruct((1, ds), F32)],
+        + [jax.ShapeDtypeStruct(GAIN, F32)],
         scratch_shapes=[pltpu.VMEM((half, vocab), BF16)],
         compiler_params=pltpu.CompilerParams(vmem_limit_bytes=SMALL),
         cost_estimate=pl.CostEstimate(
@@ -365,38 +390,29 @@
     )(*args)
 
 
-def added(kept, pieces, rows=slice(None)):
-    first, second, third = (piece[rows].astype(F32) for piece in pieces)
+def added(kept, pieces):
+    wide = kept.shape[1]
+    first, second, third = (piece[:, :wide].astype(F32) for piece in pieces)
     return (kept[...] + first) + (second + third)
 
 
-def tail_rows(gain, count):
-    high = gain.astype(BF16).astype(F32)
-    low = gain - high
-    wide = gain.shape[1] // 2
-    rows = [p[:, n * wide : (n + 1) * wide] for n in range(2) for p in (high, low)]
-    return jnp.concatenate(rows + [jnp.zeros((count - 4, wide), F32)], axis=0)
-
-
-def tail_gain(piece, first):
-    tail = piece[first : first + 16].astype(F32)
-    return jnp.concatenate([tail[0:1] + tail[1:2], tail[2:3] + tail[3:4]], axis=1)
+def added_gain(gain, pieces, wide):
+    first, second, third = (unpacked(piece[:, wide:]) for piece in pieces)
+    return (gain[...] + first) + (second + third)
 
 
 def between_a(*refs):
     kept_0, got_0, kept_1, got_1, gain = refs[0], refs[1:4], refs[4], refs[5:8], refs[8]
     kept, sends, gain_out = refs[9], refs[10:13], refs[13]
-    rows = kept_0.shape[0]
-    half = rows // 2
+    half = kept_0.shape[0] // 2
     first = added(kept_0, got_0)
-    second = added(kept_1, got_1, slice(0, rows))
-    gains = [tail_gain(piece, rows) for piece in got_1]
-    total = (gain[...] + gains[0]) + (gains[1] + gains[2])
+    second = added(kept_1, got_1)
+    total = added_gain(gain, got_1, kept_0.shape[1])
     gain_out[...] = total
-    tail = tail_rows(total, 16)
+    tail = packed(total, half)
     kept[...] = first[:half]
     for send, piece in zip(sends, (first[half:], second[:half], second[half:])):
-        send[...] = jnp.concatenate([piece, tail], axis=0).astype(BF16)
+        send[...] = jnp.concatenate([piece, tail], axis=1).astype(BF16)
 
 
 def between_b(*refs):
@@ -412,35 +428,25 @@
 def before_z(*refs):
     kept_a, got_a, kept_b, got_b, gain = refs[0], refs[1:4], refs[4], refs[5:8], refs[8]
     kept, sends, gain_out = refs[9], refs[10:13], refs[13]
-    rows = kept_a.shape[0]
+    rows, wide = kept_a.shape
     unit = rows // 4
-    total = jnp.concatenate(
-        [added(kept_a, got_a, slice(0, rows)), added(kept_b, got_b)], axis=1
-    )
-    gains = [tail_gain(piece, rows) for piece in got_a]
-    share = (gain[...] + gains[0]) + (gains[1] + gains[2])
+    total = jnp.concatenate([added(kept_a, got_a), added(kept_b, got_b)], axis=1)
+    share = added_gain(gain, got_a, wide)
     gain_out[...] = share
-    high = share.astype(BF16).astype(F32)
-    tail = jnp.concatenate(
-        [high, share - high, jnp.zeros((14 - unit, share.shape[1]), F32)], axis=0
-    )
+    tail = packed(share, unit)
     kept[...] = total[:unit]
     for send, n in zip(sends, (2, 1, 3)):
         piece = total[n * unit : (n + 1) * unit]
-        send[...] = jnp.concatenate([piece, tail], axis=0).astype(BF16)
-
-
-def last_gain(kept, first, second, third, out):
-    unit = first.shape[0] // 2
-    tails = [piece[...].astype(F32)[unit:] for piece in (first, second, third)]
-    shares = [tail[0:1] + tail[1:2] for tail in tails]
-    out[...] = (kept[...] + shares[0]) + (shares[1] + shares[2])
+        send[...] = jnp.concatenate([piece, tail], axis=1).astype(BF16)
+
+
+def last_gain(gain, first, second, third, out):
+    wide = first.shape[1] - 2 * gain.size // first.shape[0]
+    out[...] = added_gain(gain, (first, second, third), wide)
 
 
 def last_states(kept, first, second, third, states, gain, out):
-    unit = kept.shape[0]
-    pieces = [piece[...].astype(F32)[:unit] for piece in (first, second, third)]
-    total = (kept[...] + pieces[0]) + (pieces[1] + pieces[2])
+    total = added(kept, (first, second, third))
     own = states[...]
     inverse = lax.rsqrt(jnp.mean(own * own, axis=1, keepdims=True) + EPSILON)
     scaled = total * gain[...]
@@ -506,10 +512,9 @@
 
     local = jnp.concatenate([half_0[2][:2], half_1[2][:2]], axis=1)
     whole = jnp.dot(local, order, precision=lax.Precision.HIGHEST)
-    spread = jnp.broadcast_to(whole.reshape(1, 8, -1), (64, 8, half // 2))
-    every = lax.all_to_all(spread, AXES[:4], 0, 0, tiled=True)
-    top = jnp.max(every, axis=0)
-    whole = (top + jnp.log(jnp.sum(jnp.exp(every - top), axis=0))).reshape(whole.shape)
+    for axis in ("x", "y", "z"):
+        parts = [whole] + [permute(whole, moved((axis, axis), s)) for s in (1, 3, 2)]
+        whole = log_sum(parts)
     relative = jnp.dot(whole, order.T, precision=lax.Precision.HIGHEST)
     rows = jnp.concatenate([relative, weight[None], jnp.zeros((5, 2 * half), F32)], axis=0)
 
@@ -536,7 +541,7 @@
     count = half // 8
     kept_a, *sends_a, gain = small(
         between_a,
-        [((count, wide), F32)] + [((count + 16, wide), BF16)] * 3 + [((1, ds), F32)],
+        [((count, wide), F32)] + [((count, wide + 256), BF16)] * 3 + [(GAIN, F32)],
         *(kept_0, *got_0, kept_1, *got_1, gain),
     )
     got_a = exchange(sends_a, "y")
@@ -548,12 +553,12 @@
     got_b = exchange(sends_b, "x")
     kept, *sends, gain = small(
         before_z,
-        [((unit, ds), F32)] + [((16, ds), BF16)] * 3 + [((1, ds), F32)],
+        [((unit, ds), F32)] + [((unit, ds + 1024), BF16)] * 3 + [(GAIN, F32)],
         *(kept_a, *got_a, kept_b, *got_b, gain),
     )
     got = exchange(sends, "z")
-    (gain,) = small(last_gain, [((1, ds), F32)], gain, *got)
-    gain_grad = (gain + swap(gain))[0]
+    (gain,) = small(last_gain, [(GAIN, F32)], gain, *got)
+    gain_grad = (gain + swap(gain)).reshape(-1)[:ds]
     (states_grad,) = small(
         last_states, [((unit, ds), F32)], kept, *got, own_states, gain_row
     )

time: 187 us -> 178 us (0.952)
  local copies, waits for them, and re-layouts: 17.2 us -> 3.15 us
  starting transfers between devices: 45.5 us -> 49.3 us
  waiting for transfers between devices: 67.8 us -> 70 us
    unnamed x48 -> x24, local copies, waits for them, and re-layouts: 13.4 us -> 0.08 us
    ppermute x29 -> x38, starting transfers between devices: 36.4 us -> 49.3 us  [permute(): return lax.ppermute(array, AXES, pairs)]
    ppermute x29 -> x38, waiting for transfers between devices: 58.8 us -> 70 us  [permute(): return lax.ppermute(array, AXES, pairs)]
    all_to_all x1 -> x0, starting transfers between devices: 9.06 us -> none  [body(): every = lax.all_to_all(spread, AXES[:4], 0, 0, tiled=True)]
    all_to_all x1 -> x0, waiting for transfers between devices: 8.93 us -> none  [body(): every = lax.all_to_all(spread, AXES[:4], 0, 0, tiled=True)]
  transfers between devices with their start and end apart: 30 -> 38, of which waited for: 17 -> 23; matrix products, arithmetic and copies ran while one was open for 2% -> 3% of each run, Pallas kernels for 16% -> 16%
where the time goes in v1:
time: 178 us; the launch traced here: 175 us
  waiting for transfers between devices  70 us (39%)
  starting transfers between devices  49.3 us (28%)
  Pallas kernels  46.8 us (26%)
  local copies, waits for them, and re-layouts  3.15 us (2%)
  matrix products  3.01 us (2%)
    ppermute x38, waiting for transfers between devices, permute(): return lax.ppermute(array, AXES, pairs)  70 us
    ppermute x38, starting transfers between devices, permute(): return lax.ppermute(array, AXES, pairs)  49.3 us
    pallas_call x1, Pallas kernels, logits_streamed(): pl.pallas_call(functools.partial(streamed_kernel, tile), in_specs=[vmem]...  17 us
    pallas_call x1, Pallas kernels, logits(): pl.pallas_call(functools.partial(logits_kernel, tile), in_specs=[vmem] *...  12.9 us
    pallas_call x2, Pallas kernels, backward(): pl.pallas_call(functools.partial(backward_kernel, tile, later), in_specs=...  10.3 us
    pallas_call x1, Pallas kernels, resident(): pl.pallas_call(resident_kernel, in_specs=[pl.BlockSpec(memory_space=pl.AN...  5.2 us
  transfers between devices with their start and end apart: 38, of which 23 were waited for; matrix products, arithmetic and copies ran while one was open for 3% of the time, Pallas kernels for 16%

profile of v1, /device:TPU:1, one launch (start us, length us, event | category | flops | bytes accessed | tf_op | source)
XLA Modules:
  0.0 174.6 jit_solution(14521998247462025415)
XLA Ops:
  2.3 1.5 convolution_convert_fusion.1
  5.7 1.6 collective-permute-start.1
  7.4 12.0 %collective-permute-done.refs_2_ = bf16[64,8192]{1,0:T(8,128)(2,1)S(1)} collective-permute-done((bf16[64,8192]{1,0:T(8,128)(2,1)S(1)}, bf16[64,8192]{1,0:T(8,128)(2,1)S(1)}, u32[]{:S(2)}, u32[]{:S(2)}) %collective-permute-start) | collective-permute-done | bytes 1048608 | tf_op jit(solution)/shard_map/ppermute | solution.py:34
  19.3 2.3 %collective-permute-done.1.refs_1_ = bf16[64,8192]{1,0:T(8,128)(2,1)S(1)} collective-permute-done((bf16[64,8192]{1,0:T(8,128)(2,1)S(1)}, bf16[64,8192]{1,0:T(8,128)(2,1)S(1)}, u32[]{:S(2)}, u32[]{:S(2)}) %collective-permute-start.1) | collective-permute-done | bytes 1048608 | tf_op jit(solution)/shard_map/ppermute | solution.py:34
  23.0 13.6 %collective-permute-done.2.refs_0_ = bf16[64,8192]{1,0:T(8,128)(2,1)S(1)} collective-permute-done((bf16[64,8192]{1,0:T(8,128)(2,1)S(1)}, bf16[64,8192]{1,0:T(8,128)(2,1)S(1)}, u32[]{:S(2)}, u32[]{:S(2)}) %collective-permute-start.2) | collective-permute-done | bytes 1048608 | tf_op jit(solution)/shard_map/ppermute | solution.py:34
  39.6 17.0 %shard_map.77 = (f32[256,2048]{1,0:T(8,128)}, f32[256,2048]{1,0:T(8,128)}, f32[8,256]{1,0:T(8,128)}, bf16[256,3584]{1,0:T(8,128)(2,1)}) custom-call(bf16[64,8192]{1,0:T(8,128)(2,1)} %copy-done.6, bf16[64,8192]{1,0:T(8,128)(2,1)} %copy-done.8, bf16[64,8192]{1,0:T(8,128)(2,1)} %copy-done.7, bf16[64,8192]{1,0:T(8,128)(2,1)} %copy-done.9, ...), custom_call_target="tpu_custom_call" | custom-call | flops 8589934592 | bytes 33554432 | tf_op jit(solution)/shard_map/pallas_call | solution.py:225
  59.7 5.2 %shard_map.78 = (bf16[1024,3584]{1,0:T(8,128)(2,1)S(1)}, bf16[1024,3584]{1,0:T(8,128)(2,1)S(1)}) custom-call(bf16[1024,3584]{1,0:T(8,128)(2,1)} %refs_0_, bf16[1024,3584]{1,0:T(8,128)(2,1)} %collective-permute-done.7.refs_8_.refs_1_), custom_call_target="tpu_custom_call" | custom-call | bytes 29360128 | tf_op jit(solution)/shard_map/pallas_call | solution.py:90
  64.9 2.8 %collective-permute-done.9.refs_4_ = bf16[64,3584]{1,0:T(8,128)(2,1)} collective-permute-done((bf16[64,3584]{1,0:T(8,128)(2,1)}, bf16[64,3584]{1,0:T(8,128)(2,1)}, u32[]{:S(2)}, u32[]{:S(2)}) %collective-permute-start.9) | collective-permute-done | bytes 458784 | tf_op jit(solution)/shard_map/ppermute | solution.py:34
  67.8 12.9 %shard_map.79 = (f32[256,2048]{1,0:T(8,128)S(1)}, f32[256,2048]{1,0:T(8,128)S(1)}, f32[8,256]{1,0:T(8,128)S(1)}, bf16[256,3584]{1,0:T(8,128)(2,1)S(1)}) custom-call(bf16[64,8192]{1,0:T(8,128)(2,1)S(1)} %collective-permute-done.2.refs_0_, bf16[64,8192]{1,0:T(8,128)(2,1)S(1)} %collective-permute-done.5.refs_1_, ...), custom_call_target="tpu_custom_call" | custom-call | flops 8589934592 | bytes 33554432 | tf_op jit(solution)/shard_map/pallas_call | solution.py:261
  81.3 2.5 %collective-permute-start.10 = (f32[2,512]{1,0:T(2,128)S(1)}, f32[2,512]{1,0:T(2,128)S(1)}, u32[]{:S(2)}, u32[]{:S(2)}) collective-permute-start(f32[2,512]{1,0:T(2,128)S(1)} %fusion.1), channel_id=1, source_target_pairs={{0,4},{1,13},{4,8},{5,1},{8,12},{9,5},{12,0},{13,9},{16,20},{17,29... | collective-permute-start | bytes 12296 | tf_op jit(solution)/shard_map/ppermute | solution.py:34
  83.8 1.7 collective-permute-start.12
  85.5 1.9 %collective-permute-done.11 = f32[2,512]{1,0:T(2,128)S(1)} collective-permute-done((f32[2,512]{1,0:T(2,128)S(1)}, f32[2,512]{1,0:T(2,128)S(1)}, u32[]{:S(2)}, u32[]{:S(2)}) %collective-permute-start.11) | collective-permute-done | bytes 4128 | tf_op jit(solution)/shard_map/ppermute | solution.py:34
  87.7 2.0 %collective-permute-start.13 = (f32[2,512]{1,0:T(2,128)S(1)}, f32[2,512]{1,0:T(2,128)S(1)}, u32[]{:S(2)}, u32[]{:S(2)}) collective-permute-start(f32[2,512]{1,0:T(2,128)S(1)} %log_add_fusion.1), channel_id=1, source_target_pairs={{0,32},{1,97},{4,36},{5,101},{8,40},{9,105},{12,44},{13,109},{16,4... | collective-permute-start | bytes 12296 | tf_op jit(solution)/shard_map/ppermute | solution.py:34
  91.1 2.3 %collective-permute-done.14 = f32[2,512]{1,0:T(2,128)S(1)} collective-permute-done((f32[2,512]{1,0:T(2,128)S(1)}, f32[2,512]{1,0:T(2,128)S(1)}, u32[]{:S(2)}, u32[]{:S(2)}) %collective-permute-start.14) | collective-permute-done | bytes 4128 | tf_op jit(solution)/shard_map/ppermute | solution.py:34
  93.8 2.2 %collective-permute-start.16 = (f32[2,512]{1,0:T(2,128)S(1)}, f32[2,512]{1,0:T(2,128)S(1)}, u32[]{:S(2)}, u32[]{:S(2)}) collective-permute-start(f32[2,512]{1,0:T(2,128)S(1)} %log_add_fusion), channel_id=1, source_target_pairs={{0,16},{1,19},{4,20},{5,23},{8,24},{9,27},{12,28},{13,31},{16,2},{... | collective-permute-start | bytes 12296 | tf_op jit(solution)/shard_map/ppermute | solution.py:34
  95.9 2.7 %collective-permute-start.18 = (f32[2,512]{1,0:T(2,128)S(1)}, f32[2,512]{1,0:T(2,128)S(1)}, u32[]{:S(2)}, u32[]{:S(2)}) collective-permute-start(f32[2,512]{1,0:T(2,128)S(1)} %log_add_fusion), channel_id=1, source_target_pairs={{0,2},{1,3},{4,6},{5,7},{8,10},{9,11},{12,14},{13,15},{16,18},{17,... | collective-permute-start | bytes 12296 | tf_op jit(solution)/shard_map/ppermute | solution.py:34
  101.1 5.2 %shard_map.80 = (bf16[64,1792]{1,0:T(8,128)(2,1)S(1)}, bf16[64,1792]{1,0:T(8,128)(2,1)S(1)}, bf16[64,1792]{1,0:T(8,128)(2,1)S(1)}, f32[64,1792]{1,0:T(8,128)S(1)...) custom-call(f32[256,2048]{1,0:T(8,128)S(1)} %copy-done.2, ...), custom_call_target="tpu_custom_call" | custom-call | flops 3758096384 | bytes 14680064 | tf_op jit(solution)/shard_map/pallas_call | solution.py:362
  106.2 2.1 %collective-permute-start.22 = (bf16[128,1792]{1,0:T(8,128)(2,1)S(1)}, bf16[128,1792]{1,0:T(8,128)(2,1)S(1)}, u32[]{:S(2)}, u32[]{:S(2)}) collective-permute-start(bf16[128,1792]{1,0:T(8,128)(2,1)S(1)} %get-tuple-element.97), channel_id=1, source_target_pairs={{0,32},{1,97},{4,36},{5,101},{8,40},{9,105},{12,44},{13,109},{16,4... | collective-permute-start | bytes 1376264 | tf_op jit(solution)/shard_map/ppermute | solution.py:34
  108.4 2.8 %collective-permute-start.19 = (bf16[64,1792]{1,0:T(8,128)(2,1)S(1)}, bf16[64,1792]{1,0:T(8,128)(2,1)S(1)}, u32[]{:S(2)}, u32[]{:S(2)}) collective-permute-start(bf16[64,1792]{1,0:T(8,128)(2,1)S(1)} %get-tuple-element.94), channel_id=1, source_target_pairs={{0,4},{1,13},{4,8},{5,1},{8,12},{9,5},{12,0},{13,9},{16,20},{17,29... | collective-permute-start | bytes 688136 | tf_op jit(solution)/shard_map/ppermute | solution.py:34
  111.8 5.2 %shard_map.81 = (bf16[64,1920]{1,0:T(8,128)(2,1)S(1)}, bf16[64,1920]{1,0:T(8,128)(2,1)S(1)}, bf16[64,1920]{1,0:T(8,128)(2,1)S(1)}, f32[64,1792]{1,0:T(8,128)S(1)...) custom-call(f32[256,2048]{1,0:T(8,128)S(1)} %get-tuple-element.98.refs_0_, ...), custom_call_target="tpu_custom_call" | custom-call | flops 3758096384 | bytes 14680064 | tf_op jit(solution)/shard_map/pallas_call | solution.py:362
  117.7 2.1 %collective-permute-done.21.refs_3_ = bf16[64,1792]{1,0:T(8,128)(2,1)S(1)} collective-permute-done((bf16[64,1792]{1,0:T(8,128)(2,1)S(1)}, bf16[64,1792]{1,0:T(8,128)(2,1)S(1)}, u32[]{:S(2)}, u32[]{:S(2)}) %collective-permute-start.21) | collective-permute-done | bytes 229408 | tf_op jit(solution)/shard_map/ppermute | solution.py:34
  122.0 5.0 %collective-permute-done.23.refs_5_ = bf16[64,1920]{1,0:T(8,128)(2,1)S(1)} collective-permute-done((bf16[64,1920]{1,0:T(8,128)(2,1)S(1)}, bf16[64,1920]{1,0:T(8,128)(2,1)S(1)}, u32[]{:S(2)}, u32[]{:S(2)}) %collective-permute-start.23) | collective-permute-done | bytes 245792 | tf_op jit(solution)/shard_map/ppermute | solution.py:34
  127.0 3.7 %collective-permute-done.24.refs_6_ = bf16[64,1920]{1,0:T(8,128)(2,1)S(1)} collective-permute-done((bf16[64,1920]{1,0:T(8,128)(2,1)S(1)}, bf16[64,1920]{1,0:T(8,128)(2,1)S(1)}, u32[]{:S(2)}, u32[]{:S(2)}) %collective-permute-start.24) | collective-permute-done | bytes 245792 | tf_op jit(solution)/shard_map/ppermute | solution.py:34
  130.7 3.3 %collective-permute-done.25.refs_7_ = bf16[64,1920]{1,0:T(8,128)(2,1)S(1)} collective-permute-done((bf16[64,1920]{1,0:T(8,128)(2,1)S(1)}, bf16[64,1920]{1,0:T(8,128)(2,1)S(1)}, u32[]{:S(2)}, u32[]{:S(2)}) %collective-permute-start.25) | collective-permute-done | bytes 245792 | tf_op jit(solution)/shard_map/ppermute | solution.py:34
  134.2 2.4 %collective-permute-start.26 = (bf16[32,2048]{1,0:T(8,128)(2,1)S(1)}, bf16[32,2048]{1,0:T(8,128)(2,1)S(1)}, u32[]{:S(2)}, u32[]{:S(2)}) collective-permute-start(bf16[32,2048]{1,0:T(8,128)(2,1)S(1)} %get-tuple-element.116), channel_id=1, source_target_pairs={{0,32},{1,97},{4,36},{5,101},{8,40},{9,105},{12,44},{13,109},{16,4... | collective-permute-start | bytes 393224 | tf_op jit(solution)/shard_map/ppermute | solution.py:34
  138.3 1.6 collective-permute-start.31
  139.8 5.8 %collective-permute-done.26.refs_1_ = bf16[32,2048]{1,0:T(8,128)(2,1)S(1)} collective-permute-done((bf16[32,2048]{1,0:T(8,128)(2,1)S(1)}, bf16[32,2048]{1,0:T(8,128)(2,1)S(1)}, u32[]{:S(2)}, u32[]{:S(2)}) %collective-permute-start.26) | collective-permute-done | bytes 131104 | tf_op jit(solution)/shard_map/ppermute | solution.py:34
  146.5 5.3 %collective-permute-done.33.refs_7_ = bf16[32,1792]{1,0:T(8,128)(2,1)S(1)} collective-permute-done((bf16[32,1792]{1,0:T(8,128)(2,1)S(1)}, bf16[32,1792]{1,0:T(8,128)(2,1)S(1)}, u32[]{:S(2)}, u32[]{:S(2)}) %collective-permute-start.33) | collective-permute-done | bytes 114720 | tf_op jit(solution)/shard_map/ppermute | solution.py:34
  152.0 2.1 %collective-permute-start.35 = (bf16[8,4608]{1,0:T(8,128)(2,1)S(1)}, bf16[8,4608]{1,0:T(8,128)(2,1)S(1)}, u32[]{:S(2)}, u32[]{:S(2)}) collective-permute-start(bf16[8,4608]{1,0:T(8,128)(2,1)S(1)} %get-tuple-element.130), channel_id=1, source_target_pairs={{0,2},{1,3},{4,6},{5,7},{8,10},{9,11},{12,14},{13,15},{16,18},{17,... | collective-permute-start | bytes 221192 | tf_op jit(solution)/shard_map/ppermute | solution.py:34
  155.1 1.6 collective-permute-done.35.second
  156.7 1.7 collective-permute-done.36.third
  158.5 14.5 %collective-permute-start.37 = (f32[32,128]{1,0:T(8,128)S(1)}, f32[32,128]{1,0:T(8,128)S(1)}, u32[]{:S(2)}, u32[]{:S(2)}) collective-permute-start(f32[32,128]{1,0:T(8,128)S(1)} %shard_map.86), channel_id=1, source_target_pairs={{0,1},{1,0},{4,5},{5,4},{8,9},{9,8},{12,13},{13,12},{16,17},{17,16... | collective-permute-start | bytes 49160 | tf_op jit(solution)/shard_map/ppermute | solution.py:34
  (99 shorter events, 25.0 us)
Async XLA Ops:
  0.6 39.0 %collective-permute-start.6 = (bf16[1024,4608]{1,0:T(8,128)(2,1)}, bf16[1024,4608]{1,0:T(8,128)(2,1)}, u32[]{:S(2)}, u32[]{:S(2)}) collective-permute-start(bf16[1024,4608]{1,0:T(8,128)(2,1)} %refs_6_.2), channel_id=1, source_target_pairs={{0,1},{1,0},{4,5},{5,4},{8,9},{9,8},{12,13},{13,12},{16,17},{17,16... | collective-permute-start | bytes 28311560 | tf_op jit(solution)/shard_map/ppermute | solution.py:34
  2.1 37.5 %collective-permute-start.7 = (bf16[1024,3584]{1,0:T(8,128)(2,1)}, bf16[1024,3584]{1,0:T(8,128)(2,1)}, u32[]{:S(2)}, u32[]{:S(2)}) collective-permute-start(bf16[1024,3584]{1,0:T(8,128)(2,1)} %refs_0_), channel_id=1, source_target_pairs={{0,1},{1,0},{4,5},{5,4},{8,9},{9,8},{12,13},{13,12},{16,17},{17,16... | collective-permute-start | bytes 22020104 | tf_op jit(solution)/shard_map/ppermute | solution.py:34
  4.3 15.1 %collective-permute-start = (bf16[64,8192]{1,0:T(8,128)(2,1)S(1)}, bf16[64,8192]{1,0:T(8,128)(2,1)S(1)}, u32[]{:S(2)}, u32[]{:S(2)}) collective-permute-start(bf16[64,8192]{1,0:T(8,128)(2,1)S(1)} %pad_maximum_fusion.refs_0_), channel_id=1, source_target_pairs={{0,96},{1,33},{4,100},{5,37},{8,104},{9,41},{12,108},{13,45},{16,1... | collective-permute-start | bytes 3145736 | tf_op jit(solution)/shard_map/ppermute | solution.py:34
  5.7 15.9 %collective-permute-start.1 = (bf16[64,8192]{1,0:T(8,128)(2,1)S(1)}, bf16[64,8192]{1,0:T(8,128)(2,1)S(1)}, u32[]{:S(2)}, u32[]{:S(2)}) collective-permute-start(bf16[64,8192]{1,0:T(8,128)(2,1)S(1)} %pad_maximum_fusion.refs_0_), channel_id=1, source_target_pairs={{0,18},{1,17},{4,22},{5,21},{8,26},{9,25},{12,30},{13,29},{16,0},{... | collective-permute-start | bytes 3145736 | tf_op jit(solution)/shard_map/ppermute | solution.py:34
  21.7 14.9 %collective-permute-start.2 = (bf16[64,8192]{1,0:T(8,128)(2,1)S(1)}, bf16[64,8192]{1,0:T(8,128)(2,1)S(1)}, u32[]{:S(2)}, u32[]{:S(2)}) collective-permute-start(bf16[64,8192]{1,0:T(8,128)(2,1)S(1)} %collective-permute-done.refs_2_), channel_id=1, source_target_pairs={{0,96},{1,33},{4,100},{5,37},{8,104},{9,41},{12,108},{13,45},{16,1... | collective-permute-start | bytes 3145736 | tf_op jit(solution)/shard_map/ppermute | solution.py:34
  23.0 14.9 %collective-permute-start.3 = (bf16[64,8192]{1,0:T(8,128)(2,1)S(1)}, bf16[64,8192]{1,0:T(8,128)(2,1)S(1)}, u32[]{:S(2)}, u32[]{:S(2)}) collective-permute-start(bf16[64,8192]{1,0:T(8,128)(2,1)S(1)} %collective-permute-done.refs_2_), channel_id=1, source_target_pairs={{0,18},{1,17},{4,22},{5,21},{8,26},{9,25},{12,30},{13,29},{16,0},{... | collective-permute-start | bytes 3145736 | tf_op jit(solution)/shard_map/ppermute | solution.py:34
  37.8 18.8 %collective-permute-start.4 = (bf16[64,8192]{1,0:T(8,128)(2,1)S(1)}, bf16[64,8192]{1,0:T(8,128)(2,1)S(1)}, u32[]{:S(2)}, u32[]{:S(2)}) collective-permute-start(bf16[64,8192]{1,0:T(8,128)(2,1)S(1)} %collective-permute-done.2.refs_0_), channel_id=1, source_target_pairs={{0,96},{1,33},{4,100},{5,37},{8,104},{9,41},{12,108},{13,45},{16,1... | collective-permute-start | bytes 3145736 | tf_op jit(solution)/shard_map/ppermute | solution.py:34
  38.8 17.8 %collective-permute-start.5 = (bf16[64,8192]{1,0:T(8,128)(2,1)S(1)}, bf16[64,8192]{1,0:T(8,128)(2,1)S(1)}, u32[]{:S(2)}, u32[]{:S(2)}) collective-permute-start(bf16[64,8192]{1,0:T(8,128)(2,1)S(1)} %collective-permute-done.2.refs_0_), channel_id=1, source_target_pairs={{0,18},{1,17},{4,22},{5,21},{8,26},{9,25},{12,30},{13,29},{16,0},{... | collective-permute-start | bytes 3145736 | tf_op jit(solution)/shard_map/ppermute | solution.py:34
  57.5 10.3 %collective-permute-start.8 = (bf16[64,4608]{1,0:T(8,128)(2,1)}, bf16[64,4608]{1,0:T(8,128)(2,1)}, u32[]{:S(2)}, u32[]{:S(2)}) collective-permute-start(bf16[64,4608]{1,0:T(8,128)(2,1)} %slice.29), channel_id=1, source_target_pairs={{0,18},{1,17},{4,22},{5,21},{8,26},{9,25},{12,30},{13,29},{16,0},{... | collective-permute-start | bytes 1769480 | tf_op jit(solution)/shard_map/ppermute | solution.py:34
  58.7 9.0 %collective-permute-start.9 = (bf16[64,3584]{1,0:T(8,128)(2,1)}, bf16[64,3584]{1,0:T(8,128)(2,1)}, u32[]{:S(2)}, u32[]{:S(2)}) collective-permute-start(bf16[64,3584]{1,0:T(8,128)(2,1)} %slice.30), channel_id=1, source_target_pairs={{0,96},{1,33},{4,100},{5,37},{8,104},{9,41},{12,108},{13,45},{16,1... | collective-permute-start | bytes 1376264 | tf_op jit(solution)/shard_map/ppermute | solution.py:34
  81.3 4.2 %collective-permute-start.10 = (f32[2,512]{1,0:T(2,128)S(1)}, f32[2,512]{1,0:T(2,128)S(1)}, u32[]{:S(2)}, u32[]{:S(2)}) collective-permute-start(f32[2,512]{1,0:T(2,128)S(1)} %fusion.1), channel_id=1, source_target_pairs={{0,4},{1,13},{4,8},{5,1},{8,12},{9,5},{12,0},{13,9},{16,20},{17,29... | collective-permute-start | bytes 12296 | tf_op jit(solution)/shard_map/ppermute | solution.py:34
  83.8 4.0 %collective-permute-start.12 = (f32[2,512]{1,0:T(2,128)S(1)}, f32[2,512]{1,0:T(2,128)S(1)}, u32[]{:S(2)}, u32[]{:S(2)}) collective-permute-start(f32[2,512]{1,0:T(2,128)S(1)} %fusion.1), channel_id=1, source_target_pairs={{0,8},{1,9},{4,12},{5,13},{8,0},{9,1},{12,4},{13,5},{16,24},{17,25... | collective-permute-start | bytes 12296 | tf_op jit(solution)/shard_map/ppermute | solution.py:34
  93.8 5.3 %collective-permute-start.16 = (f32[2,512]{1,0:T(2,128)S(1)}, f32[2,512]{1,0:T(2,128)S(1)}, u32[]{:S(2)}, u32[]{:S(2)}) collective-permute-start(f32[2,512]{1,0:T(2,128)S(1)} %log_add_fusion), channel_id=1, source_target_pairs={{0,16},{1,19},{4,20},{5,23},{8,24},{9,27},{12,28},{13,31},{16,2},{... | collective-permute-start | bytes 12296 | tf_op jit(solution)/shard_map/ppermute | solution.py:34
  95.9 4.3 %collective-permute-start.18 = (f32[2,512]{1,0:T(2,128)S(1)}, f32[2,512]{1,0:T(2,128)S(1)}, u32[]{:S(2)}, u32[]{:S(2)}) collective-permute-start(f32[2,512]{1,0:T(2,128)S(1)} %log_add_fusion), channel_id=1, source_target_pairs={{0,2},{1,3},{4,6},{5,7},{8,10},{9,11},{12,14},{13,15},{16,18},{17,... | collective-permute-start | bytes 12296 | tf_op jit(solution)/shard_map/ppermute | solution.py:34
  106.2 13.5 %collective-permute-start.22 = (bf16[128,1792]{1,0:T(8,128)(2,1)S(1)}, bf16[128,1792]{1,0:T(8,128)(2,1)S(1)}, u32[]{:S(2)}, u32[]{:S(2)}) collective-permute-start(bf16[128,1792]{1,0:T(8,128)(2,1)S(1)} %get-tuple-element.97), channel_id=1, source_target_pairs={{0,32},{1,97},{4,36},{5,101},{8,40},{9,105},{12,44},{13,109},{16,4... | collective-permute-start | bytes 1376264 | tf_op jit(solution)/shard_map/ppermute | solution.py:34
  108.4 8.6 %collective-permute-start.19 = (bf16[64,1792]{1,0:T(8,128)(2,1)S(1)}, bf16[64,1792]{1,0:T(8,128)(2,1)S(1)}, u32[]{:S(2)}, u32[]{:S(2)}) collective-permute-start(bf16[64,1792]{1,0:T(8,128)(2,1)S(1)} %get-tuple-element.94), channel_id=1, source_target_pairs={{0,4},{1,13},{4,8},{5,1},{8,12},{9,5},{12,0},{13,9},{16,20},{17,29... | collective-permute-start | bytes 688136 | tf_op jit(solution)/shard_map/ppermute | solution.py:34
  111.2 6.5 %collective-permute-start.20 = (bf16[64,1792]{1,0:T(8,128)(2,1)S(1)}, bf16[64,1792]{1,0:T(8,128)(2,1)S(1)}, u32[]{:S(2)}, u32[]{:S(2)}) collective-permute-start(bf16[64,1792]{1,0:T(8,128)(2,1)S(1)} %get-tuple-element.95), channel_id=1, source_target_pairs={{0,8},{1,9},{4,12},{5,13},{8,0},{9,1},{12,4},{13,5},{16,24},{17,25... | collective-permute-start | bytes 688136 | tf_op jit(solution)/shard_map/ppermute | solution.py:34
  111.2 8.5 %collective-permute-start.21 = (bf16[64,1792]{1,0:T(8,128)(2,1)S(1)}, bf16[64,1792]{1,0:T(8,128)(2,1)S(1)}, u32[]{:S(2)}, u32[]{:S(2)}) collective-permute-start(bf16[64,1792]{1,0:T(8,128)(2,1)S(1)} %get-tuple-element.96), channel_id=1, source_target_pairs={{0,12},{1,5},{4,0},{5,9},{8,4},{9,13},{12,8},{13,1},{16,28},{17,21... | collective-permute-start | bytes 688136 | tf_op jit(solution)/shard_map/ppermute | solution.py:34
  119.7 17.5 %collective-permute-start.29 = (bf16[128,1792]{1,0:T(8,128)(2,1)S(1)}, bf16[128,1792]{1,0:T(8,128)(2,1)S(1)}, u32[]{:S(2)}, u32[]{:S(2)}) collective-permute-start(bf16[128,1792]{1,0:T(8,128)(2,1)S(1)} %get-tuple-element.121), channel_id=1, source_target_pairs={{0,64},{1,65},{4,68},{5,69},{8,72},{9,73},{12,76},{13,77},{16,80},... | collective-permute-start | bytes 1376264 | tf_op jit(solution)/shard_map/ppermute | solution.py:34
  119.7 18.3 %collective-permute-start.30 = (bf16[128,1792]{1,0:T(8,128)(2,1)S(1)}, bf16[128,1792]{1,0:T(8,128)(2,1)S(1)}, u32[]{:S(2)}, u32[]{:S(2)}) collective-permute-start(bf16[128,1792]{1,0:T(8,128)(2,1)S(1)} %get-tuple-element.122), channel_id=1, source_target_pairs={{0,96},{1,33},{4,100},{5,37},{8,104},{9,41},{12,108},{13,45},{16,1... | collective-permute-start | bytes 1376264 | tf_op jit(solution)/shard_map/ppermute | solution.py:34
  120.4 6.6 %collective-permute-start.23 = (bf16[64,1920]{1,0:T(8,128)(2,1)S(1)}, bf16[64,1920]{1,0:T(8,128)(2,1)S(1)}, u32[]{:S(2)}, u32[]{:S(2)}) collective-permute-start(bf16[64,1920]{1,0:T(8,128)(2,1)S(1)} %get-tuple-element.111), channel_id=1, source_target_pairs={{0,4},{1,13},{4,8},{5,1},{8,12},{9,5},{12,0},{13,9},{16,20},{17,29... | collective-permute-start | bytes 737288 | tf_op jit(solution)/shard_map/ppermute | solution.py:34
  121.2 9.6 %collective-permute-start.24 = (bf16[64,1920]{1,0:T(8,128)(2,1)S(1)}, bf16[64,1920]{1,0:T(8,128)(2,1)S(1)}, u32[]{:S(2)}, u32[]{:S(2)}) collective-permute-start(bf16[64,1920]{1,0:T(8,128)(2,1)S(1)} %get-tuple-element.112), channel_id=1, source_target_pairs={{0,8},{1,9},{4,12},{5,13},{8,0},{9,1},{12,4},{13,5},{16,24},{17,25... | collective-permute-start | bytes 737288 | tf_op jit(solution)/shard_map/ppermute | solution.py:34
  121.7 12.3 %collective-permute-start.25 = (bf16[64,1920]{1,0:T(8,128)(2,1)S(1)}, bf16[64,1920]{1,0:T(8,128)(2,1)S(1)}, u32[]{:S(2)}, u32[]{:S(2)}) collective-permute-start(bf16[64,1920]{1,0:T(8,128)(2,1)S(1)} %get-tuple-element.113), channel_id=1, source_target_pairs={{0,12},{1,5},{4,0},{5,9},{8,4},{9,13},{12,8},{13,1},{16,28},{17,21... | collective-permute-start | bytes 737288 | tf_op jit(solution)/shard_map/ppermute | solution.py:34
  134.2 11.4 %collective-permute-start.26 = (bf16[32,2048]{1,0:T(8,128)(2,1)S(1)}, bf16[32,2048]{1,0:T(8,128)(2,1)S(1)}, u32[]{:S(2)}, u32[]{:S(2)}) collective-permute-start(bf16[32,2048]{1,0:T(8,128)(2,1)S(1)} %get-tuple-element.116), channel_id=1, source_target_pairs={{0,32},{1,97},{4,36},{5,101},{8,40},{9,105},{12,44},{13,109},{16,4... | collective-permute-start | bytes 393224 | tf_op jit(solution)/shard_map/ppermute | solution.py:34
  136.6 9.1 %collective-permute-start.27 = (bf16[32,2048]{1,0:T(8,128)(2,1)S(1)}, bf16[32,2048]{1,0:T(8,128)(2,1)S(1)}, u32[]{:S(2)}, u32[]{:S(2)}) collective-permute-start(bf16[32,2048]{1,0:T(8,128)(2,1)S(1)} %get-tuple-element.117), channel_id=1, source_target_pairs={{0,64},{1,65},{4,68},{5,69},{8,72},{9,73},{12,76},{13,77},{16,80},... | collective-permute-start | bytes 393224 | tf_op jit(solution)/shard_map/ppermute | solution.py:34
  136.8 8.9 %collective-permute-start.28 = (bf16[32,2048]{1,0:T(8,128)(2,1)S(1)}, bf16[32,2048]{1,0:T(8,128)(2,1)S(1)}, u32[]{:S(2)}, u32[]{:S(2)}) collective-permute-start(bf16[32,2048]{1,0:T(8,128)(2,1)S(1)} %get-tuple-element.118), channel_id=1, source_target_pairs={{0,96},{1,33},{4,100},{5,37},{8,104},{9,41},{12,108},{13,45},{16,1... | collective-permute-start | bytes 393224 | tf_op jit(solution)/shard_map/ppermute | solution.py:34
  138.3 7.4 %collective-permute-start.31 = (bf16[32,1792]{1,0:T(8,128)(2,1)S(1)}, bf16[32,1792]{1,0:T(8,128)(2,1)S(1)}, u32[]{:S(2)}, u32[]{:S(2)}) collective-permute-start(bf16[32,1792]{1,0:T(8,128)(2,1)S(1)} %get-tuple-element.124), channel_id=1, source_target_pairs={{0,4},{1,13},{4,8},{5,1},{8,12},{9,5},{12,0},{13,9},{16,20},{17,29... | collective-permute-start | bytes 344072 | tf_op jit(solution)/shard_map/ppermute | solution.py:34
  139.8 6.7 %collective-permute-start.32 = (bf16[32,1792]{1,0:T(8,128)(2,1)S(1)}, bf16[32,1792]{1,0:T(8,128)(2,1)S(1)}, u32[]{:S(2)}, u32[]{:S(2)}) collective-permute-start(bf16[32,1792]{1,0:T(8,128)(2,1)S(1)} %get-tuple-element.125), channel_id=1, source_target_pairs={{0,8},{1,9},{4,12},{5,13},{8,0},{9,1},{12,4},{13,5},{16,24},{17,25... | collective-permute-start | bytes 344072 | tf_op jit(solution)/shard_map/ppermute | solution.py:34
  145.7 6.1 %collective-permute-start.33 = (bf16[32,1792]{1,0:T(8,128)(2,1)S(1)}, bf16[32,1792]{1,0:T(8,128)(2,1)S(1)}, u32[]{:S(2)}, u32[]{:S(2)}) collective-permute-start(bf16[32,1792]{1,0:T(8,128)(2,1)S(1)} %get-tuple-element.126), channel_id=1, source_target_pairs={{0,12},{1,5},{4,0},{5,9},{8,4},{9,13},{12,8},{13,1},{16,28},{17,21... | collective-permute-start | bytes 344072 | tf_op jit(solution)/shard_map/ppermute | solution.py:34
  152.0 4.8 %collective-permute-start.35 = (bf16[8,4608]{1,0:T(8,128)(2,1)S(1)}, bf16[8,4608]{1,0:T(8,128)(2,1)S(1)}, u32[]{:S(2)}, u32[]{:S(2)}) collective-permute-start(bf16[8,4608]{1,0:T(8,128)(2,1)S(1)} %get-tuple-element.130), channel_id=1, source_target_pairs={{0,2},{1,3},{4,6},{5,7},{8,10},{9,11},{12,14},{13,15},{16,18},{17,... | collective-permute-start | bytes 221192 | tf_op jit(solution)/shard_map/ppermute | solution.py:34
  154.0 4.4 %collective-permute-start.36 = (bf16[8,4608]{1,0:T(8,128)(2,1)S(1)}, bf16[8,4608]{1,0:T(8,128)(2,1)S(1)}, u32[]{:S(2)}, u32[]{:S(2)}) collective-permute-start(bf16[8,4608]{1,0:T(8,128)(2,1)S(1)} %get-tuple-element.131), channel_id=1, source_target_pairs={{0,18},{1,17},{4,22},{5,21},{8,26},{9,25},{12,30},{13,29},{16,0},{... | collective-permute-start | bytes 221192 | tf_op jit(solution)/shard_map/ppermute | solution.py:34
  158.5 15.3 %collective-permute-start.37 = (f32[32,128]{1,0:T(8,128)S(1)}, f32[32,128]{1,0:T(8,128)S(1)}, u32[]{:S(2)}, u32[]{:S(2)}) collective-permute-start(f32[32,128]{1,0:T(8,128)S(1)} %shard_map.86), channel_id=1, source_target_pairs={{0,1},{1,0},{4,5},{5,4},{8,9},{9,8},{12,13},{13,12},{16,17},{17,16... | collective-permute-start | bytes 49160 | tf_op jit(solution)/shard_map/ppermute | solution.py:34
  (18 other events, 304.2 us)
